TPU v7x, 512 devices: a whole 4x4x16 slice. The times are simulated.
512 devices in a mesh: span: 32 (over y, z_lo), head: 16 (over x, z_hi, core).
Axes of the slice: x: 4, y: 4, z: 16 (z_hi: 2, z_lo: 8; z = z_hi * 8 + z_lo), core: 2. Of those that a mesh axis runs over, the one named last changes fastest.
Arguments:
- query: bfloat16 [12288, 4096], P(('span', 'head'))
- keys: bfloat16 [12288, 4096], P(('span', 'head'))
- values: bfloat16 [12288, 4096], P(('span', 'head')), may hold values from -6 to 6
- out_weight: bfloat16 [4096, 5120], P('head'), may hold values from -0.5 to 0.5
- time_gates: float32 [30, 5120], replicated, may hold values from 0.5 to 2
- noise_step: int32 [32], replicated, may hold values from 0 to 29
- span_length: int32 [32], replicated, may hold values from 96 to 384, as said below
- window_start: int32 [32], replicated, may hold values from 0 to 15, as said below
- latent: float32 [12288, 5120], P(('span', 'head')), may hold values from -6 to 6
Outputs:
- velocity: bfloat16 [12288, 5120], P(('span', 'head'))
- advanced: float32 [12288, 5120], P(('span', 'head'))
Inputs may be any that keep to these rules, and one draw needn't show every extreme that they name: `span_length`: every span has at least 96 live tokens, and some span is full. window_start[c] <= c // 2 for every span c, so a span always attends to itself.
All inputs are finite; a program needn't handle non-finite values.
Results may differ from a plain program's by a relative error of at most 0.02.
Values may be sent and summed in bfloat16 or wider, within the bound.
A program may use at most 128 MiB of HBM per device.

v0:
```python
import jax
import jax.numpy as jnp
from jax import lax
from jax.sharding import PartitionSpec as P

HEADS = 32
STEPS = 30


def sigma_of(step):
    fraction = 1.0 - step.astype(jnp.float32) / STEPS
    return 8.0 * fraction / (1.0 + 7.0 * fraction)


def attend(state, key_rows, value_rows, start, query_heads, bounds):
    own_span, first_span, lengths, span_tok = bounds
    top_score, total, summed = state
    count = key_rows.shape[0]
    heads_dev = query_heads.shape[1]
    head_size = query_heads.shape[2]
    rows = start + jnp.arange(count, dtype=jnp.int32)
    owner = rows // span_tok
    position = rows % span_tok
    matches = owner[:, None] == jnp.arange(lengths.shape[0], dtype=jnp.int32)[None, :]
    key_length = jnp.sum(jnp.where(matches, lengths[None, :], 0), axis=1)
    seen = (owner >= first_span) & (owner <= own_span) & (position < key_length)
    key_heads = key_rows.reshape(count, heads_dev, head_size)
    value_heads = value_rows.reshape(count, heads_dev, head_size)
    score = jnp.einsum("qhd,khd->hqk", query_heads, key_heads, preferred_element_type=jnp.float32)
    score = score / jnp.sqrt(jnp.float32(head_size))
    masked = jnp.where(seen[None, None, :], score, jnp.float32(-1e30))
    new_top = jnp.maximum(top_score, jnp.max(masked, axis=-1))
    weight = jnp.where(seen[None, None, :], jnp.exp(score - new_top[..., None]), jnp.float32(0.0))
    factor = jnp.exp(top_score - new_top)
    total = total * factor + jnp.sum(weight, axis=-1)
    summed = summed * factor[..., None] + jnp.einsum(
        "hqk,khd->hqd", weight.astype(jnp.bfloat16), value_heads, preferred_element_type=jnp.float32
    )
    return (new_top, total, summed)


def body(
    query, keys, values, out_weight, time_gates, noise_step, span_length, window_start, latent
):
    tok_rows = query.shape[0]
    head_count = lax.axis_size("head")
    span_tok = tok_rows * head_count
    heads_dev = HEADS // head_count
    head_size = query.shape[1] // HEADS
    query_all, keys_all, values_all = (
        lax.all_to_all(query, "head", split_axis=1, concat_axis=0, tiled=True),
        lax.all_to_all(keys, "head", split_axis=1, concat_axis=0, tiled=True),
        lax.all_to_all(values, "head", split_axis=1, concat_axis=0, tiled=True),
    )
    query_heads = query_all.reshape(span_tok, heads_dev, head_size)
    own_span = lax.axis_index("span")
    first_span = lax.dynamic_index_in_dim(window_start, own_span, keepdims=False)
    bounds = (own_span, first_span, span_length, span_tok)
    empty = (
        jnp.full((heads_dev, span_tok), -1e30, jnp.float32),
        jnp.zeros((heads_dev, span_tok), jnp.float32),
        jnp.zeros((heads_dev, span_tok, head_size), jnp.float32),
    )
    keys_whole, values_whole = (
        lax.all_gather(keys_all, "span", axis=0, tiled=True),
        lax.all_gather(values_all, "span", axis=0, tiled=True),
    )
    blocks = keys_whole.shape[0] // span_tok
    keys_block = keys_whole.reshape(blocks, span_tok, keys_whole.shape[1])
    values_block = values_whole.reshape(blocks, span_tok, values_whole.shape[1])

    def scan_block(state, inputs):
        block_id, key_rows, value_rows = inputs
        return (attend(state, key_rows, value_rows, block_id * span_tok, query_heads, bounds), None)

    final_state, unused = lax.scan(
        scan_block, empty, (jnp.arange(blocks, dtype=jnp.int32), keys_block, values_block)
    )
    top_score, total, summed = final_state
    attended = (summed / total[..., None]).astype(jnp.bfloat16)
    attended = jnp.transpose(attended, (1, 0, 2)).reshape(span_tok, heads_dev * head_size)
    projected = lax.psum_scatter(
        jnp.dot(attended, out_weight, preferred_element_type=jnp.float32).astype(jnp.bfloat16),
        "head",
        scatter_dimension=0,
        tiled=True,
    ).astype(jnp.float32)
    own_step = lax.dynamic_index_in_dim(noise_step, own_span, keepdims=False)
    own_length = lax.dynamic_index_in_dim(span_length, own_span, keepdims=False)
    level_match = jnp.arange(time_gates.shape[0], dtype=jnp.int32) == own_step
    gate_row = jnp.sum(jnp.where(level_match[:, None], time_gates, jnp.float32(0.0)), axis=0)
    position = lax.axis_index("head") * tok_rows + jnp.arange(tok_rows, dtype=jnp.int32)
    live = (position < own_length).astype(jnp.float32)
    velocity = (gate_row[None, :] * projected * live[:, None]).astype(jnp.bfloat16)
    step_size = sigma_of(own_step + 1) - sigma_of(own_step)
    advanced = latent + step_size * velocity.astype(jnp.float32)
    return (velocity, advanced)


def solution(mesh):
    return jax.shard_map(
        body,
        mesh=mesh,
        in_specs=(
            P(("span", "head"), None),
            P(("span", "head"), None),
            P(("span", "head"), None),
            P("head", None),
            P(),
            P(),
            P(),
            P(),
            P(("span", "head"), None),
        ),
        out_specs=(P(("span", "head"), None), P(("span", "head"), None)),
        check_vma=False,
    )
```

profile of v0, /device:TPU:24, one launch (start us, length us, event | category | flops | bytes accessed | tf_op | source)
XLA Modules:
  0.0 1019.9 jit_solution(8027430094479857204)
XLA Ops:
  8.4 33.9 %all_to_all.54 = bf16[24,16,256]{2,0,1:T(8,128)(2,1)} all-to-all(bf16[24,16,256]{2,0,1:T(8,128)(2,1)S(1)} %bitcast.61), channel_id=1, replica_groups=mesh['span'=32,'head'=16] {'head'}, dimensions={1} | all-to-all | bytes 393216 | tf_op jit(solution)/shard_map/all_to_all | solution.py:52
  43.3 19.4 %all_to_all.55 = bf16[24,16,256]{2,0,1:T(8,128)(2,1)} all-to-all(bf16[24,16,256]{2,0,1:T(8,128)(2,1)S(1)} %bitcast.62), channel_id=1, replica_groups=mesh['span'=32,'head'=16] {'head'}, dimensions={1} | all-to-all | bytes 393216 | tf_op jit(solution)/shard_map/all_to_all | solution.py:53
  63.5 5.0 all-to-all-start.1
  69.3 17.6 %all-to-all-done.1 = bf16[24,16,256]{2,0,1:T(8,128)(2,1)S(1)} async-done(((bf16[24,16,256]{2,0,1:T(8,128)(2,1)}), bf16[24,16,256]{2,0,1:T(8,128)(2,1)S(1)}, u32[]{:S(2)}, u32[]{:S(2)}) %all-to-all-start.1) | async-done | bytes 196640 | tf_op jit(solution)/shard_map/all_to_all | solution.py:51
  87.6 190.6 %all-gather.3.cloned.1.call-done = bf16[12288,256]{1,0:T(8,128)(2,1)} async-done(((bf16[384,256]{1,0:T(8,128)(2,1)}), bf16[12288,256]{1,0:T(8,128)(2,1)}) %all-gather.3.cloned.1.call-update) | async-done | bytes 6291472 | tf_op jit(solution)/shard_map/all_gather | solution.py:65
  278.2 243.3 %all-gather.5.cloned.1.call-done = bf16[12288,256]{1,0:T(8,128)(2,1)} async-done(((bf16[384,256]{1,0:T(8,128)(2,1)}), bf16[12288,256]{1,0:T(8,128)(2,1)}) %all-gather.5.cloned.1.call-update) | async-done | bytes 6291472 | tf_op jit(solution)/shard_map/all_gather | solution.py:66
  521.5 322.0 %while.17 = (s32[]{:T(128)}, f32[2,384]{1,0:T(2,128)S(1)}, f32[2,384]{1,0:T(2,128)S(1)}, f32[2,384,128]{2,1,0:T(8,128)}, s32[32]{0:T(128)S(1)}, /*index=5*/s32[]...) while((s32[]{:T(128)}, f32[2,384]{1,0:T(2,128)S(1)}, ...), condition=%wide.region_5.6_spmd.clone, body=%wide.region_1.5_spmd.clone.sunk | while | flops 153994752 | bytes 9690997 | solution.py:76
  555.0 2.4 select_reduce_fusion.6
  565.0 2.4 select_reduce_fusion.6
  575.1 2.4 select_reduce_fusion.6
  585.2 2.4 select_reduce_fusion.6
  615.4 2.4 select_reduce_fusion.6
  625.4 2.4 select_reduce_fusion.6
  635.5 2.4 select_reduce_fusion.6
  645.5 2.4 select_reduce_fusion.6
  716.0 2.4 select_reduce_fusion.6
  726.1 2.4 select_reduce_fusion.6
  736.1 2.4 select_reduce_fusion.6
  806.6 2.4 select_reduce_fusion.6
  816.6 2.4 select_reduce_fusion.6
  826.7 2.4 select_reduce_fusion.6
  836.8 2.4 select_reduce_fusion.6
  844.7 3.1 convolution_convert_fusion
  852.5 158.7 %reduce-scatter.2.cloned.1.call-done = bf16[24,5120]{1,0:T(8,128)(2,1)} async-done(((bf16[384,5120]{1,0:T(8,128)(2,1)}), bf16[24,5120]{1,0:T(8,128)(2,1)}) %reduce-scatter.2.cloned.1.call-update) | async-done | bytes 245776 | tf_op jit(solution)/shard_map/reduce_scatter | solution.py:82
  (565 shorter events, 274.8 us)
Async XLA Ops:
  7.2 837.6 %copy-start = (bf16[256,5120]{1,0:T(8,128)(2,1)S(1)}, bf16[256,5120]{1,0:T(8,128)(2,1)}, u32[]{:S(2)}) copy-start(bf16[256,5120]{1,0:T(8,128)(2,1)} %param.14) | copy-start | bytes 7864324
  7.2 55.6 %copy-start.4 = (bf16[24,4096]{1,0:T(8,128)(2,1)S(1)}, bf16[24,4096]{1,0:T(8,128)(2,1)}, u32[]{:S(2)}) copy-start(bf16[24,4096]{1,0:T(8,128)(2,1)} %param.11) | copy-start | bytes 589828
  7.2 271.0 %all-gather.3.cloned.1.call-start = ((), (), s32[]{:S(2)}) async-start(), calls=%async_computation.4 | async-start | bytes 6488064 | tf_op jit(solution)/shard_map/all_gather | solution.py:65
  8.4 60.3 %copy-start.6 = (s32[32]{0:T(128)S(1)}, s32[32]{0:T(128)}, u32[]{:S(2)}) copy-start(s32[32]{0:T(128)} %param.18) | copy-start | bytes 388
  42.3 479.2 %all-gather.5.cloned.1.call-start = ((), (), s32[]{:S(2)}) async-start(), calls=%async_computation.5 | async-start | bytes 6488064 | tf_op jit(solution)/shard_map/all_gather | solution.py:66
  43.3 478.2 %copy-start.5 = (s32[32]{0:T(128)S(1)}, s32[32]{0:T(128)}, u32[]{:S(2)}) copy-start(s32[32]{0:T(128)} %param.17) | copy-start | bytes 388
  63.5 23.4 %all-to-all-start.1 = ((bf16[24,16,256]{2,0,1:T(8,128)(2,1)}), bf16[24,16,256]{2,0,1:T(8,128)(2,1)S(1)}, u32[]{:S(2)}, u32[]{:S(2)}) async-start(bf16[24,16,256]{2,0,1:T(8,128)(2,1)} %bitcast.37), calls=%async_computation.1 | async-start | bytes 393216 | tf_op jit(solution)/shard_map/all_to_all | solution.py:51
  68.5 942.7 %reduce-scatter.2.cloned.1.call-start = ((), (), s32[]{:S(2)}) async-start(), calls=%async_computation.6 | async-start | bytes 4177920 | tf_op jit(solution)/shard_map/reduce_scatter | solution.py:82
  557.4 1.8 copy-start.1
  587.6 1.8 copy-start.1
  597.6 1.8 copy-start.1
  607.7 1.8 copy-start.1
  617.7 1.8 copy-start.1
  627.8 1.8 copy-start.1
  637.9 1.8 copy-start.1
  688.2 1.8 copy-start.1
  698.2 1.8 copy-start.1
  708.3 1.8 copy-start.1
  718.4 1.8 copy-start.1
  728.4 1.8 copy-start.1
  778.8 1.8 copy-start.1
  788.8 1.8 copy-start.1
  798.9 1.8 copy-start.1
  847.8 4.5 copy-start.3
  (50 other events, 54.4 us)
Sparse Core Ops, SparseCore 0:
  42.5 235.7 all-gather.2
  280.3 241.1 all-gather.4
  848.0 163.2 reduce-scatter.1
where the time goes:
time: 1020 us
  waiting for transfers between devices  610 us (60%)
  matrix products  140 us (14%)
  local copies, waits for them, and re-layouts  94.1 us (9%)
  other arithmetic  79.8 us (8%)
  blocking collectives  53.4 us (5%)
  loops' own time  22.5 us (2%)
  between operations  15.3 us (2%)
    all_gather x1, waiting for transfers between devices, body(): lax.all_gather(values_all, 'span', axis=0, tiled=True)  243 us
    all_gather x1, waiting for transfers between devices, body(): lax.all_gather(keys_all, 'span', axis=0, tiled=True)  191 us
    reduce_scatter x1, waiting for transfers between devices, body(): lax.psum_scatter(jnp.dot(attended, out_weight, preferred_element_type=jnp...  159 us
    dot_general x32, matrix products, attend(): jnp.einsum('qhd,khd->hqk', query_heads, key_heads, preferred_element_type...  76.1 us
    dynamic_slice x128, local copies, waits for them, and re-layouts, body(): lax.scan(scan_block, empty, (jnp.arange(blocks, dtype=jnp.int32), keys_bl...  63.5 us
    dot_general x32, matrix products, attend(): jnp.einsum('hqk,khd->hqd', weight.astype(jnp.bfloat16), value_heads, pref...  60.3 us
    reduce_sum x32, other arithmetic, attend(): total = total * factor + jnp.sum(weight, axis=-1)  49.5 us
    all_to_all x1, blocking collectives, body(): lax.all_to_all(keys, 'head', split_axis=1, concat_axis=0, tiled=True)  33.9 us
  transfers between devices with their start and end apart: 4, of which 4 were waited for; matrix products, arithmetic and copies ran while one was open for 1% of the time, Pallas kernels for 0%

commit v1 on v0

v1 whole, which is shorter than its diff:
```python
import functools
import math

import jax
import jax.numpy as jnp
from jax import lax
from jax.experimental import pallas as pl
from jax.experimental.pallas import tpu as pltpu
from jax.sharding import PartitionSpec as P

MESH = pl.DeviceIdType.MESH
F32 = jnp.float32
BF16 = jnp.bfloat16

D = 5120
HS = 128
STEPS = 30
ROWS = 24
HALF = 192
NH = 4
NQ = 4 * HALF
NZ = 16
CHUNK = 640
PIECE = 64
NP = 4
TILE = 256
NEG = -1e30
BIG = 3e38
SCALE = math.log2(math.e) / math.sqrt(HS)


def place(x, y, z, core):
    return (y * 8 + z % 8, 4 * x + 2 * (z // 8) + core)


def main_kernel(
    q_ref, k_ref, v_ref, w_ref, slen_ref, wstart_ref, out_ref,
    send_a, recv_a, stage, kv, qbuf, qt, acc, stat, pos_ref, row_ref, wf,
    obuf, robuf, sbuf, rsbuf, att, fs, send_c, recv_c, send_x, recv_x,
    a_s, a_r, q_s, q_r, ring_s, ring_r, wz_s, wz_r, wy_s, wy_r, o_s, o_r, st_s, st_r, c_s, c_r, x_s, x_r,
):
    span = lax.axis_index("span")
    head = lax.axis_index("head")
    y, zlo = span // 8, span % 8
    x, zhi, core = head // 4, (head // 2) % 2, head % 2
    z = zhi * 8 + zlo
    me = core * 4 + x

    def peer(p):
        return place(p % 4, y, z, p // 4)

    def copy(src, dst, ssem, rsem, dev):
        return pltpu.make_async_remote_copy(
            src_ref=src, dst_ref=dst, send_sem=ssem, recv_sem=rsem, device_id=dev, device_id_type=MESH
        )

    side = (place(x, y, (z + 1) % NZ, core), place(x, y, (z + NZ - 1) % NZ, core))

    def ydev(d):
        return place(x, (y + d) % 4, z, core)

    barrier = pltpu.get_barrier_semaphore()
    partners = [peer((me + d) % 8) for d in range(1, 8)] + [ydev(d) for d in range(1, 4)] + list(side)
    for dev in partners:
        pl.semaphore_signal(barrier, inc=1, device_id=dev, device_id_type=MESH)

    def pack(p, carry):
        for tensor, ref in enumerate((q_ref, k_ref, v_ref)):
            for l in range(NH):
                col = 128 * (8 * (p % 4) + 4 * (l // 2) + 2 * (p // 4) + l % 2)
                stage[0, pl.ds((tensor * NH + l) * ROWS, ROWS), :] = ref[
                    :, pl.ds(pl.multiple_of(col, 128), 128)
                ].astype(F32)
        send_a[p] = stage[0, pl.ds(0, 12 * ROWS), :].astype(BF16)
        return carry

    lax.fori_loop(0, 8, pack, 0)
    pl.semaphore_wait(barrier, len(partners))

    def a_copy(d):
        to = (me + d) % 8
        return copy(send_a.at[to], recv_a.at[me], a_s.at[d - 1], a_r.at[d - 1], peer(to))

    def a_start(d, carry):
        a_copy(d).start()
        return carry

    lax.fori_loop(1, 8, a_start, 0)

    def wz_forward(direction, i):
        c = 2 * y + direction
        rows = pl.ds(pl.multiple_of(i * PIECE, PIECE), PIECE)
        return copy(
            wf.at[c, rows], wf.at[c, rows], wz_s.at[direction, i], wz_r.at[direction, i], side[direction]
        )

    def wz_origin(direction, i):
        c = 2 * y + direction
        rows = pl.ds(pl.multiple_of(i * PIECE, PIECE), PIECE)
        cols = pl.ds(pl.multiple_of(c * CHUNK, 128), CHUNK)
        return copy(
            w_ref.at[rows, cols], wf.at[c, rows], wz_s.at[direction, i], wz_r.at[direction, i], side[direction]
        )

    def wy_copy(direction, i, d):
        c = 2 * y + direction
        rows = pl.ds(pl.multiple_of(i * PIECE, PIECE), PIECE)
        return copy(
            wf.at[c, rows], wf.at[c, rows], wy_s.at[direction, i, d - 1], wy_r.at[direction, i, d - 1], ydev(d)
        )

    for direction in range(2):

        @pl.when(zlo == (7 if direction == 0 else 0))
        def _(direction=direction):
            def go(i, carry):
                wz_origin(direction, i).start()
                return carry

            lax.fori_loop(0, NP, go, 0)

    def weight_point(u):
        for direction in range(2):
            hop = zlo if direction == 0 else 7 - zlo
            i = u - hop

            @pl.when((i >= 0) & (i < NP))
            def _(direction=direction, hop=hop, i=i):
                wz_forward(direction, i).wait_recv()

                @pl.when(hop < 7)
                def _():
                    wz_forward(direction, i).start()

                for d in range(1, 4):
                    wy_copy(direction, i, d).start()

    r = lax.broadcasted_iota(jnp.int32, (HALF, 128), 0)
    rc = jnp.where(r >= 96, 1, 0)
    rem = r - 96 * rc
    rx = jnp.where(rem >= 24, 1, 0) + jnp.where(rem >= 48, 1, 0) + jnp.where(rem >= 72, 1, 0)
    pos_ref[...] = 96 * rx + 24 * rc + rem - 24 * rx
    lane = lax.broadcasted_iota(jnp.int32, (8, NQ), 1)
    ly = jnp.where(lane >= HALF, 1, 0) + jnp.where(lane >= 2 * HALF, 1, 0) + jnp.where(lane >= 3 * HALF, 1, 0)
    row_ref[0] = 8 * ly + zlo
    first = jnp.full((8, NQ), wstart_ref[zlo], jnp.int32)
    for yy in range(1, 4):
        first = jnp.where(ly == yy, wstart_ref[8 * yy + zlo], first)
    row_ref[1] = first
    acc[...] = jnp.zeros(acc.shape, F32)
    stat[pl.ds(0, 4), :] = jnp.full((4, 1024), NEG, F32)
    stat[pl.ds(4, 4), :] = jnp.zeros((4, 1024), F32)

    recv_a[me] = send_a[me]

    def unpack(d, carry):
        src = (me + 8 - d) % 8

        @pl.when(d > 0)
        def _():
            a_copy_in(d).wait_recv()

        rows = recv_a[src].astype(F32)
        at = pl.ds(pl.multiple_of(src * ROWS, 8), ROWS)
        for tensor in range(3):
            for l in range(NH):
                n = (tensor * NH + l) * ROWS
                stage[tensor * NH + l, at, :] = rows[n : n + ROWS]
        return carry

    def a_copy_in(d):
        src = (me + 8 - d) % 8
        return copy(send_a.at[src], recv_a.at[src], a_s.at[d - 1], a_r.at[d - 1], peer(src))

    lax.fori_loop(0, 8, unpack, 0)

    def ring_copy(direction, ab, n):
        block = (z + NZ - (n - 1)) % NZ if direction == 0 else (z + n - 1) % NZ
        ref = kv.at[(direction + ab) % 2, block]
        return copy(ref, ref, ring_s.at[direction, ab, n - 1], ring_r.at[direction, ab, n - 1], side[direction])

    def ring_in(direction, ab, n):
        block = (z + NZ - n) % NZ if direction == 0 else (z + n) % NZ
        ref = kv.at[(direction + ab) % 2, block]
        return copy(ref, ref, ring_s.at[direction, ab, n - 1], ring_r.at[direction, ab, n - 1], side[direction])

    for tensor in range(2):
        for l in range(NH):
            kv[tensor, z, pl.ds(l * HALF, HALF), :] = stage[(tensor + 1) * NH + l, pl.ds(0, HALF), :].astype(BF16)
        ring_copy(0, tensor, 1).start()
        ring_copy(1, 1 - tensor, 1).start()
    for l in range(NH):
        qbuf[y, pl.ds(l * HALF, HALF), :] = stage[l, pl.ds(0, HALF), :].astype(BF16)

    def q_copy(d):
        return copy(qbuf.at[y], qbuf.at[y], q_s.at[d - 1], q_r.at[d - 1], ydev(4 - d))

    def q_in(d):
        src = (y + d) % 4
        return copy(qbuf.at[src], qbuf.at[src], q_s.at[d - 1], q_r.at[d - 1], ydev(d))

    for d in range(1, 4):

        @pl.when(y - d >= 0)
        def _(d=d):
            q_copy(d).start()
            qbuf[y - d] = jnp.zeros((NQ, 128), BF16)

    def point(ab, n, last, u):
        for direction in range(2):
            ring_in(direction, ab, n).wait_recv()

            @pl.when(n < last)
            def _(direction=direction):
                ring_copy(direction, ab, n + 1).start()

        weight_point(u)

    for d in range(1, 4):

        @pl.when(y + d <= 3)
        def _(d=d):
            q_in(d).wait_recv()

    def turn(l, carry):
        rows = pl.ds(pl.multiple_of(l * HALF, 64), HALF)
        q_all = jnp.concatenate([qbuf[yy, rows, :].astype(F32) for yy in range(4)], axis=0)
        qt[l] = q_all.T.astype(BF16)
        return carry

    lax.fori_loop(0, NH, turn, 0)
    point(0, 1, 8, 0)
    point(1, 1, 7, 1)

    def attend(za, zb, low, high):
        sides = []
        for zz in (za, zb):
            j = 8 * y + zz % 8
            cap = jnp.where(pos_ref[...] + 48 * (zz // 8) < slen_ref[j], BIG, NEG).astype(F32)
            cap = jnp.concatenate([cap, cap], axis=1)
            seen = (row_ref[1] <= j) & (j <= row_ref[0])
            sides.append((zz, cap, seen))

        def one_head(l, carry):
            rows = pl.ds(pl.multiple_of(l * HALF, 64), HALF)
            k2 = jnp.concatenate([kv[0, za, rows, :], kv[0, zb, rows, :]], axis=0)
            v2 = jnp.concatenate([kv[1, za, rows, :], kv[1, zb, rows, :]], axis=0).T
            for tile in range(NQ // TILE):
                cols = pl.ds(tile * TILE, TILE)
                s = jnp.dot(k2, qt[l, :, cols], preferred_element_type=F32) * SCALE
                old = stat[pl.ds(l, 1), cols]
                top = old
                parts = []
                for n, (zz, cap, seen) in enumerate(sides):
                    part = jnp.minimum(s[n * HALF : (n + 1) * HALF], cap)
                    vis = seen[0:1, tile * TILE : (tile + 1) * TILE]
                    top = jnp.maximum(top, jnp.where(vis, jnp.max(part, axis=0, keepdims=True), NEG))
                    parts.append((part, vis))
                factor = jnp.exp2(old - top)
                weight = jnp.concatenate(
                    [jnp.exp2(part - jnp.where(vis, top, BIG)) for part, vis in parts], axis=0
                )
                stat[pl.ds(l, 1), cols] = top
                stat[pl.ds(4 + l, 1), cols] = stat[pl.ds(4 + l, 1), cols] * factor + jnp.sum(
                    weight, axis=0, keepdims=True
                )
                acc[l, :, cols] = acc[l, :, cols] * factor + jnp.dot(
                    v2, weight.astype(BF16), preferred_element_type=F32
                )
            return carry

        lax.fori_loop(low, high, one_head, 0)

    def step(t, carry):
        za, zb = (z + NZ - t) % NZ, (z + t) % NZ
        point(0, t + 1, 8, 2 * t)
        attend(za, zb, 0, 2)

        @pl.when(t < 7)
        def _():
            point(1, t + 1, 7, 2 * t + 1)

        attend(za, zb, 2, 4)
        return carry

    lax.fori_loop(1, 8, step, 0)
    attend(z, (z + 8) % NZ, 0, 4)

    def finish(l, carry):
        inv = 1.0 / jnp.maximum(stat[pl.ds(4 + l, 1), pl.ds(0, NQ)], 1e-30)
        o = (acc[l] * inv).T.astype(BF16)
        rows = pl.ds(pl.multiple_of(l * HALF, 64), HALF)
        for yy in range(4):
            obuf[yy, rows, :] = o[yy * HALF : (yy + 1) * HALF]
        return carry

    lax.fori_loop(0, NH, finish, 0)
    stats = stat[...]
    for yy in range(4):
        sbuf[yy] = stats[:, yy * HALF : yy * HALF + 256]

    def o_copy(d):
        to = (y + d) % 4
        return (
            copy(sbuf.at[to], rsbuf.at[y], st_s.at[d - 1], st_r.at[d - 1], ydev(d)),
            copy(obuf.at[to], robuf.at[y], o_s.at[d - 1], o_r.at[d - 1], ydev(d)),
        )

    def o_in(d):
        src = (y + 4 - d) % 4
        return (
            copy(sbuf.at[src], rsbuf.at[src], st_s.at[d - 1], st_r.at[d - 1], ydev(4 - d)),
            copy(obuf.at[src], robuf.at[src], o_s.at[d - 1], o_r.at[d - 1], ydev(4 - d)),
        )

    empty = jnp.where(lax.broadcasted_iota(jnp.int32, (8, 256), 0) < 4, NEG, 0.0).astype(F32)
    for d in range(1, 4):

        @pl.when(y + d <= 3)
        def _(d=d):
            for one in o_copy(d):
                one.start()
            rsbuf[y + d] = empty
            robuf[y + d] = jnp.zeros((NQ, 128), BF16)

    rsbuf[y] = sbuf[y]
    robuf[y] = obuf[y]
    for d in range(1, 4):

        @pl.when(y - d >= 0)
        def _(d=d):
            for one in o_in(d):
                one.wait_recv()

    tops = [rsbuf[yy, pl.ds(0, 4), :] for yy in range(4)]
    best = jnp.maximum(jnp.maximum(tops[0], tops[1]), jnp.maximum(tops[2], tops[3]))
    shares = [rsbuf[yy, pl.ds(4, 4), :] * jnp.exp2(tops[yy] - best) for yy in range(4)]
    whole = shares[0] + shares[1] + shares[2] + shares[3]
    inv = 1.0 / whole
    share = jnp.concatenate([one * inv for one in shares] + [jnp.zeros((112, 256), F32)], axis=0).T
    for l in range(NH):
        o = jnp.zeros((HALF, HS), F32)
        for yy in range(4):
            n = 4 * yy + l
            o = o + share[0:HALF, n : n + 1] * robuf[yy, pl.ds(l * HALF, HALF), :].astype(F32)
        att[l // 2, :, pl.ds((l % 2) * HS, HS)] = o.astype(BF16)

    def wy_wait(n, carry):
        direction, i = n // NP, n % NP
        rows = pl.ds(pl.multiple_of(i * PIECE, PIECE), PIECE)
        for d in range(1, 4):
            c = 2 * ((y + 4 - d) % 4) + direction
            copy(
                wf.at[c, rows], wf.at[c, rows], wy_s.at[direction, i, d - 1], wy_r.at[direction, i, d - 1], ydev(d)
            ).wait_recv()
        return carry

    lax.fori_loop(0, 2 * NP, wy_wait, 0)
    twin = place(x, y, z, 1 - core)

    def c_copy(n):
        return copy(send_c.at[n], recv_c.at[n], c_s.at[n], c_r.at[n], twin)

    def project(n, carry):
        cols = pl.ds(pl.multiple_of(n * CHUNK, 128), CHUNK)
        fs[n] = jnp.dot(att[zhi], w_ref[:, cols], preferred_element_type=F32) + jnp.dot(
            att[1 - zhi], wf[n], preferred_element_type=F32
        )
        send_c[n] = fs[n, pl.ds(pl.multiple_of(96 * (1 - core), 8), 96), :].astype(BF16)
        c_copy(n).start()
        return carry

    lax.fori_loop(0, 8, project, 0)

    def x_copy(g, d):
        to = (x + d) % 4
        return copy(
            send_x.at[g, to], recv_x.at[g, x], x_s.at[g, d - 1], x_r.at[g, d - 1], place(to, y, z, core)
        )

    def x_in(g, d):
        src = (x + 4 - d) % 4
        return copy(
            send_x.at[g, src], recv_x.at[g, src], x_s.at[g, d - 1], x_r.at[g, d - 1], place(src, y, z, core)
        )

    def pair_sum(g, carry):
        own = pl.ds(pl.multiple_of(96 * core, 8), 96)
        parts = []
        for n in range(2):
            c_copy(2 * g + n).wait_recv()
            parts.append(fs[2 * g + n, own, :] + recv_c[2 * g + n].astype(F32))
        for xx in range(4):
            send_x[g, xx] = jnp.concatenate([part[xx * ROWS : (xx + 1) * ROWS] for part in parts], axis=0).astype(BF16)
        for d in (2, 1, 3):
            x_copy(g, d).start()
        return carry

    lax.fori_loop(0, 4, pair_sum, 0)

    def collect(g, carry):
        total = send_x[g, x].astype(F32)
        for d in range(1, 4):
            x_in(g, d).wait_recv()
            total = total + recv_x[g, (x + 4 - d) % 4].astype(F32)
        for n in range(2):
            out_ref[:, pl.ds(pl.multiple_of((2 * g + n) * CHUNK, 128), CHUNK)] = total[n * ROWS : (n + 1) * ROWS]
        return carry

    lax.fori_loop(0, 4, collect, 0)

    def a_end(d, carry):
        a_copy(d).wait_send()
        return carry

    lax.fori_loop(1, 8, a_end, 0)

    def ring_end(n, carry):
        for direction in range(2):
            ring_copy(direction, 0, n).wait_send()

            @pl.when(n < 8)
            def _(direction=direction):
                ring_copy(direction, 1, n).wait_send()

        return carry

    lax.fori_loop(1, 9, ring_end, 0)

    def w_end(i, carry):
        for direction in range(2):
            wz_forward(direction, i).wait_send()
            for d in range(1, 4):
                wy_copy(direction, i, d).wait_send()
        return carry

    lax.fori_loop(0, NP, w_end, 0)
    for d in range(1, 4):

        @pl.when(y - d >= 0)
        def _(d=d):
            q_copy(d).wait_send()

        @pl.when(y + d <= 3)
        def _(d=d):
            for one in o_copy(d):
                one.wait_send()

    def c_end(n, carry):
        c_copy(n).wait_send()
        return carry

    lax.fori_loop(0, 8, c_end, 0)

    def x_end(g, carry):
        for d in range(1, 4):
            x_copy(g, d).wait_send()
        return carry

    lax.fori_loop(0, 4, x_end, 0)


def last_kernel(proj_ref, gate_ref, lat_ref, step_ref, len_ref, vel_ref, adv_ref):
    span = lax.axis_index("span")
    head = lax.axis_index("head")
    level = step_ref[span]
    length = len_ref[span]

    def sigma_of(step):
        fraction = 1.0 - step / STEPS
        return 8.0 * fraction / (1.0 + 7.0 * fraction)

    now = jnp.full((ROWS, 128), level, jnp.int32).astype(F32)
    dt = sigma_of(now + 1.0) - sigma_of(now)
    spot = head * ROWS + lax.broadcasted_iota(jnp.int32, (ROWS, 128), 0)
    live = jnp.where(spot < length, 1.0, 0.0).astype(F32)
    wide = 512
    dt_w = jnp.concatenate([dt] * (wide // 128), axis=1)
    live_w = jnp.concatenate([live] * (wide // 128), axis=1)
    for n in range(D // wide):
        cols = pl.ds(n * wide, wide)
        gate = gate_ref[pl.ds(level, 1), cols]
        vel = (gate * proj_ref[:, cols] * live_w).astype(BF16)
        vel_ref[:, cols] = vel
        adv_ref[:, cols] = lat_ref[:, cols] + dt_w * vel.astype(F32)


def body(query, keys, values, out_weight, time_gates, noise_step, span_length, window_start, latent):
    vmem = pl.BlockSpec(memory_space=pltpu.VMEM)
    smem = pl.BlockSpec(memory_space=pltpu.SMEM)
    dma = pltpu.SemaphoreType.DMA
    projected = pl.pallas_call(
        main_kernel,
        out_shape=jax.ShapeDtypeStruct((ROWS, D), F32),
        in_specs=[vmem, vmem, vmem, vmem, smem, smem],
        out_specs=vmem,
        scratch_shapes=[
            pltpu.VMEM((8, 12 * ROWS, 128), BF16),
            pltpu.VMEM((8, 12 * ROWS, 128), BF16),
            pltpu.VMEM((12, 12 * ROWS, 128), F32),
            pltpu.VMEM((2, NZ, NQ, 128), BF16),
            pltpu.VMEM((4, NQ, 128), BF16),
            pltpu.VMEM((NH, HS, NQ), BF16),
            pltpu.VMEM((NH, HS, NQ), F32),
            pltpu.VMEM((8, 1024), F32),
            pltpu.VMEM((HALF, 128), jnp.int32),
            pltpu.VMEM((2, 8, NQ), jnp.int32),
            pltpu.VMEM((8, 256, CHUNK), BF16),
            pltpu.VMEM((4, NQ, 128), BF16),
            pltpu.VMEM((4, NQ, 128), BF16),
            pltpu.VMEM((4, 8, 256), F32),
            pltpu.VMEM((4, 8, 256), F32),
            pltpu.VMEM((2, HALF, 256), BF16),
            pltpu.VMEM((8, HALF, CHUNK), F32),
            pltpu.VMEM((8, 96, CHUNK), BF16),
            pltpu.VMEM((8, 96, CHUNK), BF16),
            pltpu.VMEM((4, 4, 48, CHUNK), BF16),
            pltpu.VMEM((4, 4, 48, CHUNK), BF16),
            dma((7,)), dma((7,)),
            dma((3,)), dma((3,)),
            dma((2, 2, 8)), dma((2, 2, 8)),
            dma((2, NP)), dma((2, NP)),
            dma((2, NP, 3)), dma((2, NP, 3)),
            dma((3,)), dma((3,)),
            dma((3,)), dma((3,)),
            dma((8,)), dma((8,)),
            dma((4, 3)), dma((4, 3)),
        ],
        compiler_params=pltpu.CompilerParams(
            collective_id=0, has_side_effects=True, vmem_limit_bytes=56 * 1024 * 1024
        ),
        name="attention_tick",
    )(query, keys, values, out_weight, span_length, window_start)
    return pl.pallas_call(
        last_kernel,
        out_shape=(jax.ShapeDtypeStruct((ROWS, D), BF16), jax.ShapeDtypeStruct((ROWS, D), F32)),
        in_specs=[vmem, vmem, vmem, smem, smem],
        out_specs=(vmem, vmem),
        compiler_params=pltpu.CompilerParams(vmem_limit_bytes=32 * 1024 * 1024),
        name="euler_update",
    )(projected, time_gates, latent, noise_step, span_length)


def solution(mesh):
    rows = P(("span", "head"), None)
    return jax.shard_map(
        body,
        mesh=mesh,
        in_specs=(rows, rows, rows, P("head", None), P(), P(), P(), P(), rows),
        out_specs=(rows, rows),
        check_vma=False,
    )
```

time: 1020 us -> 146 us (0.14)
  the two profiles are of different devices: /device:TPU:24 before, /device:TPU:16 now
where the time goes in v1:
time: 146 us
  Pallas kernels  144 us (99%)
    pallas_call x1, Pallas kernels, body(): pl.pallas_call(main_kernel, out_shape=jax.ShapeDtypeStruct((ROWS, D), F32...  142 us

profile of v1, /device:TPU:16, one launch (start us, length us, event | category | flops | bytes accessed | tf_op | source)
XLA Modules:
  0.0 145.7 jit_solution(15147661468533760735)
XLA Ops:
  0.6 0.0 copy-start.3
  0.6 0.0 copy-start.2
  0.7 0.0 copy-start.4
  0.7 0.0 copy-start.1
  0.7 142.4 %attention_tick.1.proj_ref = f32[24,5120]{1,0:T(8,128)} custom-call(bf16[24,4096]{1,0:T(8,128)(2,1)} %q_ref.1, bf16[24,4096]{1,0:T(8,128)(2,1)} %k_ref.1, bf16[24,4096]{1,0:T(8,128)(2,1)} %v_ref.1, bf16[256,5120]{1,0:T(8,128)(2,1)} %w_ref.1, s32[32]{0:T(128)} %len_ref.1, s32[32]{0:T(128)} %wstart_ref.1), custom_call_target="tpu_custom_call" | custom-call | tf_op jit(solution)/shard_map/attention_tick/pallas_call | solution.py:492
  143.1 0.0 copy-done.3
  143.1 0.0 copy-done.2
  143.1 0.0 copy-done.4
  143.1 0.0 copy-done.1
  143.1 0.0 copy-start
  143.1 1.0 copy-done
  144.1 1.5 %euler_update.1 = (bf16[24,5120]{1,0:T(8,128)(2,1)}, f32[24,5120]{1,0:T(8,128)}) custom-call(f32[24,5120]{1,0:T(8,128)S(1)} %copy-done, f32[30,5120]{1,0:T(8,128)S(1)} %copy-done.1, f32[24,5120]{1,0:T(8,128)S(1)} %copy-done.2, s32[32]{0:T(128)S(1)} %copy-done.4, s32[32]{0:T(128)S(1)} %copy-done.3), custom_call_target="tpu_custom_call" | custom-call | tf_op jit(solution)/shard_map/euler_update/pallas_call | solution.py:534
Async XLA Ops:
  0.6 142.4 %copy-start.3 = (s32[32]{0:T(128)S(1)}, s32[32]{0:T(128)}, u32[]{:S(2)}) copy-start(s32[32]{0:T(128)} %len_ref.1) | copy-start | bytes 388
  0.6 142.4 %copy-start.2 = (f32[24,5120]{1,0:T(8,128)S(1)}, f32[24,5120]{1,0:T(8,128)}, u32[]{:S(2)}) copy-start(f32[24,5120]{1,0:T(8,128)} %lat_ref.1) | copy-start | bytes 1474564
  0.7 142.4 %copy-start.4 = (s32[32]{0:T(128)S(1)}, s32[32]{0:T(128)}, u32[]{:S(2)}) copy-start(s32[32]{0:T(128)} %step_ref.1) | copy-start | bytes 388
  0.7 142.4 %copy-start.1 = (f32[30,5120]{1,0:T(8,128)S(1)}, f32[30,5120]{1,0:T(8,128)}, u32[]{:S(2)}) copy-start(f32[30,5120]{1,0:T(8,128)} %gate_ref.1) | copy-start | bytes 1843204
  143.1 1.0 copy-start

commit v2 on v1

v2 whole, which is shorter than its diff:
```python
import functools
import math

import jax
import jax.numpy as jnp
from jax import lax
from jax.experimental import pallas as pl
from jax.experimental.pallas import tpu as pltpu
from jax.sharding import PartitionSpec as P

MESH = pl.DeviceIdType.MESH
F32 = jnp.float32
BF16 = jnp.bfloat16

D = 5120
HS = 128
STEPS = 30
ROWS = 24
HALF = 192
NQ = 768
NZ = 16
CHUNK = 640
PIECE = 64
NP = 4
TILE = 256
NEG = -1e30
BIG = 3e38
SCALE = math.log2(math.e) / math.sqrt(HS)


def place(x, y, z, core):
    return (y * 8 + z % 8, 4 * x + 2 * (z // 8) + core)


def main_kernel(
    q_ref, k_ref, v_ref, w_ref, slen_ref, wstart_ref, out_ref,
    pack, ex_s, ex_r, stage, send_q, send_kv, kv, vt, qbuf, qt, acc, stat, pos_ref, row_ref, wf,
    robuf, rstat, obuf, send_o, att, fs, send_c, recv_c, send_x, recv_x,
    ex_ss, ex_rs, zq_s, zq_r, zk_s, zk_r, xk_s, xk_r, q_s, q_r, wz_s, wz_r, wy_s, wy_r,
    o_s, o_r, st_s, st_r, a_s, a_r, c_s, c_r, x_s, x_r,
):
    span = lax.axis_index("span")
    head = lax.axis_index("head")
    y, zlo = span // 8, span % 8
    x, zhi, core = head // 4, (head // 2) % 2, head % 2
    z = zhi * 8 + zlo
    quad = z // 4

    def copy(src, dst, ssem, rsem, dev):
        return pltpu.make_async_remote_copy(
            src_ref=src, dst_ref=dst, send_sem=ssem, recv_sem=rsem, device_id=dev, device_id_type=MESH
        )

    def zdev(d):
        return place(x, y, (z + d) % NZ, core)

    def ydev(d):
        return place(x, (y + d) % 4, z, core)

    def xdev(d):
        return place((x + d) % 4, y, z, core)

    twin = place(x, y, z, 1 - core)

    barrier = pltpu.get_barrier_semaphore()

    def greet(dev):
        pl.semaphore_signal(barrier, inc=1, device_id=dev, device_id_type=MESH)

    greet(twin)
    for d in range(1, 4):
        greet(ydev(d))
        greet(xdev(d))

    def greet_z(d, carry):
        greet(zdev(d))
        return carry

    lax.fori_loop(1, NZ, greet_z, 0)

    def greet_o(n, carry):
        sx, sz = n // 4, 4 * x + n % 4

        @pl.when((sx != x) | (sz != z))
        def _():
            greet(place(sx, y, sz, core))

        return carry

    lax.fori_loop(0, NZ, greet_o, 0)

    def pack_tensor(ref, slot):
        def one(n, carry):
            col = 128 * (8 * (n // 4) + 4 * ((n // 2) % 2) + n % 2)
            row = pl.ds(pl.multiple_of(n * ROWS, 8), ROWS)
            theirs = ref[:, pl.ds(pl.multiple_of(col + 256 * (1 - core), 128), 128)]
            pack[row, :] = theirs.astype(F32)
            mine = ref[:, pl.ds(pl.multiple_of(col + 256 * core, 128), 128)]
            stage[slot, pl.ds(pl.multiple_of(n * 48 + core * ROWS, 8), ROWS), :] = mine.astype(F32)
            return carry

        lax.fori_loop(0, NZ, one, 0)
        ex_s[slot] = pack[...].astype(BF16)

    def ex_copy(slot):
        return copy(ex_s.at[slot], ex_r.at[slot], ex_ss.at[slot], ex_rs.at[slot], twin)

    def unpack_tensor(slot):
        ex_copy(slot).wait_recv()
        pack[...] = ex_r[slot].astype(F32)

        def one(n, carry):
            stage[slot, pl.ds(pl.multiple_of(n * 48 + (1 - core) * ROWS, 8), ROWS), :] = pack[
                pl.ds(pl.multiple_of(n * ROWS, 8), ROWS), :
            ]
            return carry

        lax.fori_loop(0, NZ, one, 0)
        return stage[slot].astype(BF16)

    pack_tensor(q_ref, 0)
    pl.semaphore_wait(barrier, 1 + 3 + 3 + 15 + 16 - jnp.where(quad == x, 1, 0))
    ex_copy(0).start()
    pack_tensor(k_ref, 1)
    ex_copy(1).start()
    pack_tensor(v_ref, 2)
    ex_copy(2).start()

    side = (zdev(1), zdev(NZ - 1))

    def wz_forward(direction, i):
        c = 2 * y + direction
        rows = pl.ds(pl.multiple_of(i * PIECE, PIECE), PIECE)
        return copy(
            wf.at[c, rows], wf.at[c, rows], wz_s.at[direction, i], wz_r.at[direction, i], side[direction]
        )

    def wz_origin(direction, i):
        c = 2 * y + direction
        rows = pl.ds(pl.multiple_of(i * PIECE, PIECE), PIECE)
        cols = pl.ds(pl.multiple_of(c * CHUNK, 128), CHUNK)
        return copy(
            w_ref.at[rows, cols], wf.at[c, rows], wz_s.at[direction, i], wz_r.at[direction, i], side[direction]
        )

    def wy_copy(direction, i, d):
        c = 2 * y + direction
        rows = pl.ds(pl.multiple_of(i * PIECE, PIECE), PIECE)
        return copy(
            wf.at[c, rows], wf.at[c, rows], wy_s.at[direction, i, d - 1], wy_r.at[direction, i, d - 1], ydev(d)
        )

    def weight_start():
        for direction in range(2):

            @pl.when(zlo == (7 if direction == 0 else 0))
            def _(direction=direction):
                def go(i, carry):
                    wz_origin(direction, i).start()
                    return carry

                lax.fori_loop(0, NP, go, 0)

    def weight_point(u):
        for direction in range(2):
            hop = zlo if direction == 0 else 7 - zlo
            i = u - hop

            @pl.when((i >= 0) & (i < NP))
            def _(direction=direction, hop=hop, i=i):
                wz_forward(direction, i).wait_recv()

                @pl.when(hop < 7)
                def _():
                    wz_forward(direction, i).start()

                for d in range(1, 4):
                    wy_copy(direction, i, d).start()

    def zrows(n):
        return pl.ds(pl.multiple_of(n * 48, 16), 48)

    def zq_copy(d):
        to = (z + d) % NZ
        return copy(send_q.at[zrows(to)], qbuf.at[y, zrows(z)], zq_s.at[d - 1], zq_r.at[d - 1], zdev(d))

    def zq_in(d):
        src = (z + NZ - d) % NZ
        return copy(send_q.at[zrows(src)], qbuf.at[y, zrows(src)], zq_s.at[d - 1], zq_r.at[d - 1], zdev(d))

    def zk_copy(d):
        to = (z + d) % NZ
        return copy(
            send_kv.at[:, zrows(to)], kv.at[:, z, zrows(x)], zk_s.at[d - 1], zk_r.at[d - 1], zdev(d)
        )

    def zk_in(d):
        src = (z + NZ - d) % NZ
        return copy(
            send_kv.at[:, zrows(src)], kv.at[:, src, zrows(x)], zk_s.at[d - 1], zk_r.at[d - 1], zdev(d)
        )

    def start_both_ways(what):
        def one(t, carry):
            what(t).start()
            what(NZ - t).start()
            return carry

        lax.fori_loop(1, 8, one, 0)
        what(8).start()

    send_q[...] = unpack_tensor(0)
    start_both_ways(zq_copy)
    qbuf[y, zrows(z), :] = send_q[zrows(z), :]
    send_kv[0] = unpack_tensor(1)
    send_kv[1] = unpack_tensor(2)
    start_both_ways(zk_copy)
    for tensor in range(2):
        kv[tensor, z, zrows(x), :] = send_kv[tensor, zrows(z), :]
    weight_start()

    def xk_copy(n, d):
        part = kv.at[:, n, zrows(x)]
        return copy(part, part, xk_s.at[n, d - 1], xk_r.at[n, d - 1], xdev(d))

    def xk_in(n, d):
        part = kv.at[:, n, zrows((x + 4 - d) % 4)]
        return copy(part, part, xk_s.at[n, d - 1], xk_r.at[n, d - 1], xdev(d))

    def spread(n):
        for d in (2, 1, 3):
            xk_copy(n, d).start()

    def spread_pair(t):
        zk_in(t).wait_recv()
        spread((z + NZ - t) % NZ)

        @pl.when(t < 8)
        def _():
            zk_in(NZ - t).wait_recv()
            spread((z + t) % NZ)

    def gathered(n):
        for d in range(1, 4):
            xk_in(n, d).wait_recv()

    spread(z)

    r = lax.broadcasted_iota(jnp.int32, (HALF, 128), 0)
    rx = jnp.where(r >= 48, 1, 0) + jnp.where(r >= 96, 1, 0) + jnp.where(r >= 144, 1, 0)
    pos_ref[...] = r + 48 * rx
    lane = lax.broadcasted_iota(jnp.int32, (8, NQ), 1)
    lz = jnp.zeros((8, NQ), jnp.int32)
    for n in range(1, NZ):
        lz = lz + jnp.where(lane >= 48 * n, 1, 0)
    lz = lz - jnp.where(lz >= 8, 8, 0)
    row_ref[4] = lz

    def first_rows(yy, carry):
        first = jnp.full((8, NQ), wstart_ref[8 * yy], jnp.int32)
        for n in range(1, 8):
            first = jnp.where(lz == n, wstart_ref[8 * yy + n], first)
        row_ref[yy] = first
        stat[yy] = jnp.where(lax.broadcasted_iota(jnp.int32, (8, NQ), 0) < 1, NEG, 0.0).astype(F32)
        acc[yy] = jnp.zeros((HS, NQ), F32)
        return carry

    lax.fori_loop(0, 4, first_rows, 0)

    def zq_wait(d, carry):
        zq_in(d).wait_recv()
        return carry

    lax.fori_loop(1, NZ, zq_wait, 0)

    def q_copy(d):
        return copy(qbuf.at[y], qbuf.at[y], q_s.at[d - 1], q_r.at[d - 1], ydev(4 - d))

    def q_in(d):
        src = (y + d) % 4
        return copy(qbuf.at[src], qbuf.at[src], q_s.at[d - 1], q_r.at[d - 1], ydev(d))

    for d in range(1, 4):

        @pl.when(y - d >= 0)
        def _(d=d):
            q_copy(d).start()

    weight_point(0)
    spread_pair(1)
    weight_point(1)
    spread_pair(2)
    weight_point(2)
    spread_pair(3)

    def turn(yy):
        qt[yy] = qbuf[yy].astype(F32).T.astype(BF16)

    turn(y)
    for d in range(1, 4):

        @pl.when(y + d <= 3)
        def _(d=d):
            q_in(d).wait_recv()
            turn(y + d)

    def blocks(t):
        return (z + NZ - t) % NZ, jnp.where(t == 8, z, (z + t) % NZ)

    def attend(t, low, high):
        sides = []
        for n in blocks(t):
            j = 8 * y + n % 8
            cap = jnp.where(pos_ref[...] + 48 * (n // 8) < slen_ref[j], BIG, NEG).astype(F32)
            sides.append((j, jnp.concatenate([cap, cap], axis=1)))
        za, zb = blocks(t)
        k2 = jnp.concatenate([kv[0, za], kv[0, zb]], axis=0)
        v2 = vt[t - 1]

        def one_row(yy, carry):
            rows = [(row_ref[yy] <= j) & (j <= 8 * yy + row_ref[4]) for j, cap in sides]
            for tile in range(NQ // TILE):
                cols = pl.ds(tile * TILE, TILE)
                s = jnp.dot(k2, qt[yy, :, cols], preferred_element_type=F32) * SCALE
                old = stat[yy, pl.ds(0, 1), cols]
                top = old
                parts = []
                for n in range(2):
                    part = jnp.minimum(s[n * HALF : (n + 1) * HALF], sides[n][1])
                    vis = rows[n][0:1, tile * TILE : (tile + 1) * TILE]
                    top = jnp.maximum(top, jnp.where(vis, jnp.max(part, axis=0, keepdims=True), NEG))
                    parts.append((part, vis))
                factor = jnp.exp2(old - top)
                weight = jnp.concatenate(
                    [jnp.exp2(part - jnp.where(vis, top, BIG)) for part, vis in parts], axis=0
                )
                stat[yy, pl.ds(0, 1), cols] = top
                stat[yy, pl.ds(1, 1), cols] = stat[yy, pl.ds(1, 1), cols] * factor + jnp.sum(
                    weight, axis=0, keepdims=True
                )
                acc[yy, :, cols] = acc[yy, :, cols] * factor + jnp.dot(
                    v2, weight.astype(BF16), preferred_element_type=F32
                )
            return carry

        lax.fori_loop(low, high, one_row, 0)

    def finished(yy):
        return (acc[yy] * (1.0 / jnp.maximum(stat[yy, pl.ds(1, 1), :], 1e-30))).astype(BF16)

    def o_copy(yy, d):
        return (
            copy(stat.at[yy], rstat.at[y], st_s.at[d - 1], st_r.at[d - 1], place(x, yy, z, core)),
            copy(obuf.at[yy], robuf.at[y], o_s.at[d - 1], o_r.at[d - 1], place(x, yy, z, core)),
        )

    def o_in(d):
        src = (y + 4 - d) % 4
        return (
            copy(stat.at[src], rstat.at[src], st_s.at[d - 1], st_r.at[d - 1], ydev(4 - d)),
            copy(obuf.at[src], robuf.at[src], o_s.at[d - 1], o_r.at[d - 1], ydev(4 - d)),
        )

    def give(yy):
        @pl.when(yy == y)
        def _():
            robuf[yy] = finished(yy)
            rstat[yy] = stat[yy]

        for d in range(1, 4):

            @pl.when(y + d == yy)
            def _(d=d):
                obuf[yy] = finished(yy)
                for one in o_copy(yy, d):
                    one.start()

    def first_pass(t, carry):
        @pl.when(t < 6)
        def _():
            spread_pair(t + 3)

        weight_point(2 * t + 1)
        for n in blocks(t):
            gathered(n)
        za, zb = blocks(t)
        vt[t - 1] = jnp.concatenate([kv[1, za], kv[1, zb]], axis=0).T
        attend(t, jnp.maximum(y, 2), 4)
        weight_point(2 * t + 2)
        return carry

    lax.fori_loop(1, 9, first_pass, 0)
    give(3)
    give(2)
    for yy in (1, 0):

        @pl.when(y <= yy)
        def _(yy=yy):
            def one(t, carry):
                attend(t, yy, yy + 1)
                return carry

            lax.fori_loop(1, 9, one, 0)
            give(yy)

    for d in range(1, 4):

        @pl.when(y + d <= 3)
        def _(d=d):
            rstat[y + d] = jnp.where(lax.broadcasted_iota(jnp.int32, (8, NQ), 0) < 1, NEG, 0.0).astype(F32)
            robuf[y + d] = jnp.zeros((HS, NQ), BF16)

        @pl.when(y - d >= 0)
        def _(d=d):
            for one in o_in(d):
                one.wait_recv()

    tops = [rstat[yy, pl.ds(0, 1), :] for yy in range(4)]
    best = jnp.maximum(jnp.maximum(tops[0], tops[1]), jnp.maximum(tops[2], tops[3]))
    shares = [rstat[yy, pl.ds(1, 1), :] * jnp.exp2(tops[yy] - best) for yy in range(4)]
    inv = 1.0 / (shares[0] + shares[1] + shares[2] + shares[3])
    mixed = jnp.zeros((HS, NQ), F32)
    for yy in range(4):
        mixed = mixed + robuf[yy].astype(F32) * (shares[yy] * inv)
    send_o[...] = mixed.T.astype(BF16)

    def a_copy(n):
        return copy(
            send_o.at[zrows(n)], att.at[z % 4, zrows(x)], a_s.at[n], a_r.at[x * 4 + z % 4], place(quad, y, n, core)
        )

    def a_in(n):
        sx = n // 4
        return copy(
            send_o.at[zrows(n)], att.at[n % 4, zrows(sx)], a_s.at[n], a_r.at[n], place(sx, y, 4 * x + n % 4, core)
        )

    def a_send(n, carry):
        to = (z + n) % NZ

        @pl.when((to != z) | (quad != x))
        def _():
            a_copy(to).start()

        return carry

    lax.fori_loop(0, NZ, a_send, 0)

    @pl.when(quad == x)
    def _():
        att[z % 4, zrows(x), :] = send_o[zrows(z), :]

    def wy_wait(n, carry):
        direction, i = n // NP, n % NP
        rows = pl.ds(pl.multiple_of(i * PIECE, PIECE), PIECE)
        for d in range(1, 4):
            c = 2 * ((y + 4 - d) % 4) + direction
            copy(
                wf.at[c, rows], wf.at[c, rows], wy_s.at[direction, i, d - 1], wy_r.at[direction, i, d - 1], ydev(d)
            ).wait_recv()
        return carry

    lax.fori_loop(0, 2 * NP, wy_wait, 0)

    def a_wait(n, carry):
        @pl.when((n // 4 != x) | (4 * x + n % 4 != z))
        def _():
            a_in(n).wait_recv()

        return carry

    lax.fori_loop(0, NZ, a_wait, 0)

    def c_copy(n):
        return copy(send_c.at[n], recv_c.at[n], c_s.at[n], c_r.at[n], twin)

    def core_rows(n, c):
        return jnp.concatenate(
            [fs[n, pl.ds(pl.multiple_of(xx * 48 + c * ROWS, 8), ROWS), :] for xx in range(4)], axis=0
        )

    def project(n):
        cols = pl.ds(pl.multiple_of(n * CHUNK, 128), CHUNK)
        near = jnp.concatenate([att[2 * zhi], att[2 * zhi + 1]], axis=1)
        far = jnp.concatenate([att[2 - 2 * zhi], att[3 - 2 * zhi]], axis=1)
        fs[n] = jnp.dot(near, w_ref[:, cols], preferred_element_type=F32) + jnp.dot(
            far, wf[n], preferred_element_type=F32
        )
        send_c[n] = core_rows(n, 1 - core).astype(BF16)
        c_copy(n).start()

    def x_copy(g, d):
        to = (x + d) % 4
        return copy(
            send_x.at[g, to], recv_x.at[g, x], x_s.at[g, d - 1], x_r.at[g, d - 1], xdev(d)
        )

    def x_in(g, d):
        src = (x + 4 - d) % 4
        return copy(
            send_x.at[g, src], recv_x.at[g, src], x_s.at[g, d - 1], x_r.at[g, d - 1], xdev(d)
        )

    def pair_sum(g):
        parts = []
        for n in range(2):
            c_copy(2 * g + n).wait_recv()
            parts.append(core_rows(2 * g + n, core) + recv_c[2 * g + n].astype(F32))
        for xx in range(4):
            send_x[g, xx] = jnp.concatenate([part[xx * ROWS : (xx + 1) * ROWS] for part in parts], axis=0).astype(BF16)
        for d in (2, 1, 3):
            x_copy(g, d).start()

    def output_step(g, carry):
        @pl.when(g < 4)
        def _():
            project(2 * g)
            project(2 * g + 1)

        @pl.when(g > 0)
        def _():
            pair_sum(g - 1)

        return carry

    lax.fori_loop(0, 5, output_step, 0)

    def collect(g, carry):
        total = send_x[g, x].astype(F32)
        for d in range(1, 4):
            x_in(g, d).wait_recv()
            total = total + recv_x[g, (x + 4 - d) % 4].astype(F32)
        for n in range(2):
            out_ref[:, pl.ds(pl.multiple_of((2 * g + n) * CHUNK, 128), CHUNK)] = total[n * ROWS : (n + 1) * ROWS]
        return carry

    lax.fori_loop(0, 4, collect, 0)

    for slot in range(3):
        ex_copy(slot).wait_send()

    def z_end(d, carry):
        zq_copy(d).wait_send()
        zk_copy(d).wait_send()
        return carry

    lax.fori_loop(1, NZ, z_end, 0)

    def n_end(n, carry):
        for d in range(1, 4):
            xk_copy(n, d).wait_send()

        @pl.when((n != z) | (quad != x))
        def _():
            a_copy(n).wait_send()

        return carry

    lax.fori_loop(0, NZ, n_end, 0)

    def w_end(i, carry):
        for direction in range(2):
            wz_forward(direction, i).wait_send()
            for d in range(1, 4):
                wy_copy(direction, i, d).wait_send()
        return carry

    lax.fori_loop(0, NP, w_end, 0)
    for d in range(1, 4):

        @pl.when(y - d >= 0)
        def _(d=d):
            q_copy(d).wait_send()

        @pl.when(y + d <= 3)
        def _(d=d):
            for one in o_copy(y + d, d):
                one.wait_send()

    def c_end(n, carry):
        c_copy(n).wait_send()
        return carry

    lax.fori_loop(0, 8, c_end, 0)

    def x_end(g, carry):
        for d in range(1, 4):
            x_copy(g, d).wait_send()
        return carry

    lax.fori_loop(0, 4, x_end, 0)


def last_kernel(proj_ref, gate_ref, lat_ref, step_ref, len_ref, vel_ref, adv_ref):
    span = lax.axis_index("span")
    head = lax.axis_index("head")
    level = step_ref[span]
    length = len_ref[span]

    def sigma_of(step):
        fraction = 1.0 - step / STEPS
        return 8.0 * fraction / (1.0 + 7.0 * fraction)

    now = jnp.full((ROWS, 128), level, jnp.int32).astype(F32)
    dt = sigma_of(now + 1.0) - sigma_of(now)
    spot = head * ROWS + lax.broadcasted_iota(jnp.int32, (ROWS, 128), 0)
    live = jnp.where(spot < length, 1.0, 0.0).astype(F32)
    wide = 512
    dt_w = jnp.concatenate([dt] * (wide // 128), axis=1)
    live_w = jnp.concatenate([live] * (wide // 128), axis=1)
    for n in range(D // wide):
        cols = pl.ds(n * wide, wide)
        gate = gate_ref[pl.ds(level, 1), cols]
        vel = (gate * proj_ref[:, cols] * live_w).astype(BF16)
        vel_ref[:, cols] = vel
        adv_ref[:, cols] = lat_ref[:, cols] + dt_w * vel.astype(F32)


def body(query, keys, values, out_weight, time_gates, noise_step, span_length, window_start, latent):
    vmem = pl.BlockSpec(memory_space=pltpu.VMEM)
    smem = pl.BlockSpec(memory_space=pltpu.SMEM)
    dma = pltpu.SemaphoreType.DMA
    projected = pl.pallas_call(
        main_kernel,
        out_shape=jax.ShapeDtypeStruct((ROWS, D), F32),
        in_specs=[vmem, vmem, vmem, vmem, smem, smem],
        out_specs=vmem,
        scratch_shapes=[
            pltpu.VMEM((NZ * ROWS, 128), F32),
            pltpu.VMEM((3, NZ * ROWS, 128), BF16),
            pltpu.VMEM((3, NZ * ROWS, 128), BF16),
            pltpu.VMEM((3, NQ, 128), F32),
            pltpu.VMEM((NQ, 128), BF16),
            pltpu.VMEM((2, NQ, 128), BF16),
            pltpu.VMEM((2, NZ, HALF, 128), BF16),
            pltpu.VMEM((8, HS, 2 * HALF), BF16),
            pltpu.VMEM((4, NQ, 128), BF16),
            pltpu.VMEM((4, HS, NQ), BF16),
            pltpu.VMEM((4, HS, NQ), F32),
            pltpu.VMEM((4, 8, NQ), F32),
            pltpu.VMEM((HALF, 128), jnp.int32),
            pltpu.VMEM((5, 8, NQ), jnp.int32),
            pltpu.VMEM((8, 256, CHUNK), BF16),
            pltpu.VMEM((4, HS, NQ), BF16),
            pltpu.VMEM((4, 8, NQ), F32),
            pltpu.VMEM((4, HS, NQ), BF16),
            pltpu.VMEM((NQ, 128), BF16),
            pltpu.VMEM((4, HALF, 128), BF16),
            pltpu.VMEM((8, HALF, CHUNK), F32),
            pltpu.VMEM((8, 96, CHUNK), BF16),
            pltpu.VMEM((8, 96, CHUNK), BF16),
            pltpu.VMEM((4, 4, 48, CHUNK), BF16),
            pltpu.VMEM((4, 4, 48, CHUNK), BF16),
            dma((3,)), dma((3,)),
            dma((15,)), dma((15,)),
            dma((15,)), dma((15,)),
            dma((NZ, 3)), dma((NZ, 3)),
            dma((3,)), dma((3,)),
            dma((2, NP)), dma((2, NP)),
            dma((2, NP, 3)), dma((2, NP, 3)),
            dma((3,)), dma((3,)),
            dma((3,)), dma((3,)),
            dma((NZ,)), dma((NZ,)),
            dma((8,)), dma((8,)),
            dma((4, 3)), dma((4, 3)),
        ],
        compiler_params=pltpu.CompilerParams(
            collective_id=0, has_side_effects=True, vmem_limit_bytes=40 * 1024 * 1024
        ),
        name="attention_tick",
    )(query, keys, values, out_weight, span_length, window_start)
    return pl.pallas_call(
        last_kernel,
        out_shape=(jax.ShapeDtypeStruct((ROWS, D), BF16), jax.ShapeDtypeStruct((ROWS, D), F32)),
        in_specs=[vmem, vmem, vmem, smem, smem],
        out_specs=(vmem, vmem),
        compiler_params=pltpu.CompilerParams(vmem_limit_bytes=32 * 1024 * 1024),
        name="euler_update",
    )(projected, time_gates, latent, noise_step, span_length)


def solution(mesh):
    rows = P(("span", "head"), None)
    return jax.shard_map(
        body,
        mesh=mesh,
        in_specs=(rows, rows, rows, P("head", None), P(), P(), P(), P(), rows),
        out_specs=(rows, rows),
        check_vma=False,
    )
```

time: 146 us -> 153 us (1.048)
  the two profiles are of different devices: /device:TPU:16 before, /device:TPU:1 now
where the time goes in v2:
time: 153 us
  Pallas kernels  146 us (95%)
  local copies, waits for them, and re-layouts  5.83 us (4%)
    pallas_call x1, Pallas kernels, body(): pl.pallas_call(main_kernel, out_shape=jax.ShapeDtypeStruct((ROWS, D), F32...  145 us
    unnamed x18, local copies, waits for them, and re-layouts  5.83 us

profile of v2, /device:TPU:1, one launch (start us, length us, event | category | flops | bytes accessed | tf_op | source)
XLA Modules:
  0.0 152.5 jit_solution(3569714887095221056)
XLA Ops:
  0.6 0.0 copy-start
  0.6 1.7 %copy-done = bf16[256,5120]{1,0:T(8,128)(2,1)S(1)} copy-done((bf16[256,5120]{1,0:T(8,128)(2,1)S(1)}, bf16[256,5120]{1,0:T(8,128)(2,1)}, u32[]{:S(2)}) %copy-start) | copy-done | bytes 2621464
  2.4 0.0 copy-start.3
  2.4 0.9 copy-done.3
  3.3 0.0 copy-start.4
  3.3 0.9 copy-done.4
  4.2 0.0 copy-start.5
  4.2 0.9 copy-done.5
  5.2 0.0 copy-start.6
  5.2 0.7 copy-done.6
  5.8 0.0 copy-start.7
  5.8 0.7 copy-done.7
  6.5 0.0 copy-start.1
  6.5 0.0 copy-start.2
  6.5 0.0 copy-start.8
  6.5 144.5 %attention_tick.1.proj_ref = f32[24,5120]{1,0:T(8,128)S(1)} custom-call(bf16[24,4096]{1,0:T(8,128)(2,1)S(1)} %copy-done.3, bf16[24,4096]{1,0:T(8,128)(2,1)S(1)} %copy-done.4, bf16[24,4096]{1,0:T(8,128)(2,1)S(1)} %copy-done.5, bf16[256,5120]{1,0:T(8,128)(2,1)S(1)} %copy-done, s32[32]{0:T(128)S(1)} %copy-done.6, s32[32]{0:T(128)S(1)} %copy-done.7), custom_call_target="tpu_custom_call" | custom-call | tf_op jit(solution)/shard_map/attention_tick/pallas_call | solution.py:623
  151.0 0.0 copy-done.1
  151.0 0.0 copy-done.2
  151.0 0.0 copy-done.8
  151.0 1.5 euler_update.1
Async XLA Ops:
  0.6 1.7 %copy-start = (bf16[256,5120]{1,0:T(8,128)(2,1)S(1)}, bf16[256,5120]{1,0:T(8,128)(2,1)}, u32[]{:S(2)}) copy-start(bf16[256,5120]{1,0:T(8,128)(2,1)} %w_ref.1) | copy-start | bytes 7864324
  2.4 0.9 copy-start.3
  3.3 0.9 copy-start.4
  4.2 0.9 copy-start.5
  5.2 0.7 copy-start.6
  5.8 0.7 copy-start.7
  6.5 144.5 %copy-start.1 = (f32[30,5120]{1,0:T(8,128)S(1)}, f32[30,5120]{1,0:T(8,128)}, u32[]{:S(2)}) copy-start(f32[30,5120]{1,0:T(8,128)} %gate_ref.1) | copy-start | bytes 1843204
  6.5 144.5 %copy-start.2 = (f32[24,5120]{1,0:T(8,128)S(1)}, f32[24,5120]{1,0:T(8,128)}, u32[]{:S(2)}) copy-start(f32[24,5120]{1,0:T(8,128)} %lat_ref.1) | copy-start | bytes 1474564
  6.5 144.5 %copy-start.8 = (s32[32]{0:T(128)S(1)}, s32[32]{0:T(128)}, u32[]{:S(2)}) copy-start(s32[32]{0:T(128)} %step_ref.1) | copy-start | bytes 388

commit v3 on v2

--- a/solution.py
+++ b/solution.py
@@ -23,6 +23,8 @@
 PIECE = 64
 NP = 4
 TILE = 256
+VT = HS + 16
+ACC = HS + 8
 NEG = -1e30
 BIG = 3e38
 SCALE = math.log2(math.e) / math.sqrt(HS)
@@ -262,7 +264,7 @@
             first = jnp.where(lz == n, wstart_ref[8 * yy + n], first)
         row_ref[yy] = first
         stat[yy] = jnp.where(lax.broadcasted_iota(jnp.int32, (8, NQ), 0) < 1, NEG, 0.0).astype(F32)
-        acc[yy] = jnp.zeros((HS, NQ), F32)
+        acc[yy] = jnp.zeros((ACC, NQ), F32)
         return carry
 
     lax.fori_loop(0, 4, first_rows, 0)
@@ -297,12 +299,6 @@
         qt[yy] = qbuf[yy].astype(F32).T.astype(BF16)
 
     turn(y)
-    for d in range(1, 4):
-
-        @pl.when(y + d <= 3)
-        def _(d=d):
-            q_in(d).wait_recv()
-            turn(y + d)
 
     def blocks(t):
         return (z + NZ - t) % NZ, jnp.where(t == 8, z, (z + t) % NZ)
@@ -319,34 +315,35 @@
 
         def one_row(yy, carry):
             rows = [(row_ref[yy] <= j) & (j <= 8 * yy + row_ref[4]) for j, cap in sides]
-            for tile in range(NQ // TILE):
-                cols = pl.ds(tile * TILE, TILE)
-                s = jnp.dot(k2, qt[yy, :, cols], preferred_element_type=F32) * SCALE
-                old = stat[yy, pl.ds(0, 1), cols]
-                top = old
+            olds = stat[yy, pl.ds(0, 1), :]
+            tiles = [slice(n * TILE, (n + 1) * TILE) for n in range(NQ // TILE)]
+            scores = [jnp.dot(k2, qt[yy, :, cols], preferred_element_type=F32) for cols in tiles]
+            tops, sums = [], []
+            for cols, s in zip(tiles, scores):
+                top = olds[:, cols]
                 parts = []
                 for n in range(2):
-                    part = jnp.minimum(s[n * HALF : (n + 1) * HALF], sides[n][1])
-                    vis = rows[n][0:1, tile * TILE : (tile + 1) * TILE]
+                    part = jnp.minimum(s[n * HALF : (n + 1) * HALF] * SCALE, sides[n][1])
+                    vis = rows[n][0:1, cols]
                     top = jnp.maximum(top, jnp.where(vis, jnp.max(part, axis=0, keepdims=True), NEG))
                     parts.append((part, vis))
-                factor = jnp.exp2(old - top)
                 weight = jnp.concatenate(
-                    [jnp.exp2(part - jnp.where(vis, top, BIG)) for part, vis in parts], axis=0
+                    [jnp.exp2(part - jnp.where(vis, top, BIG)).astype(BF16) for part, vis in parts], axis=0
                 )
+                tops.append(top)
+                sums.append(jnp.dot(v2, weight, preferred_element_type=F32))
+            for cols, top, part in zip(tiles, tops, sums):
+                factor = jnp.exp2(olds[:, cols] - top)
+                acc[yy, :, cols] = acc[yy, :, cols] * factor + part[:ACC]
                 stat[yy, pl.ds(0, 1), cols] = top
-                stat[yy, pl.ds(1, 1), cols] = stat[yy, pl.ds(1, 1), cols] * factor + jnp.sum(
-                    weight, axis=0, keepdims=True
-                )
-                acc[yy, :, cols] = acc[yy, :, cols] * factor + jnp.dot(
-                    v2, weight.astype(BF16), preferred_element_type=F32
-                )
             return carry
 
         lax.fori_loop(low, high, one_row, 0)
 
     def finished(yy):
-        return (acc[yy] * (1.0 / jnp.maximum(stat[yy, pl.ds(1, 1), :], 1e-30))).astype(BF16)
+        total = acc[yy, pl.ds(HS, 1), :]
+        stat[yy, pl.ds(1, 1), :] = total
+        return (acc[yy, pl.ds(0, HS), :] * (1.0 / jnp.maximum(total, 1e-30))).astype(BF16)
 
     def o_copy(yy, d):
         return (
@@ -384,25 +381,37 @@
         for n in blocks(t):
             gathered(n)
         za, zb = blocks(t)
-        vt[t - 1] = jnp.concatenate([kv[1, za], kv[1, zb]], axis=0).T
-        attend(t, jnp.maximum(y, 2), 4)
+        vt[t - 1, pl.ds(0, HS), :] = jnp.concatenate([kv[1, za], kv[1, zb]], axis=0).T
+        vt[t - 1, pl.ds(HS, VT - HS), :] = jnp.ones((VT - HS, 2 * HALF), BF16)
+        attend(t, y, y + 1)
         weight_point(2 * t + 2)
         return carry
 
     lax.fori_loop(1, 9, first_pass, 0)
+    for d in range(1, 4):
+
+        @pl.when(y + d <= 3)
+        def _(d=d):
+            q_in(d).wait_recv()
+            turn(y + d)
+
+    def later_pass(low, high):
+        def one(t, carry):
+            attend(t, low, high)
+            return carry
+
+        lax.fori_loop(1, 9, one, 0)
+
+    later_pass(jnp.maximum(y + 1, 2), 4)
     give(3)
     give(2)
-    for yy in (1, 0):
-
-        @pl.when(y <= yy)
-        def _(yy=yy):
-            def one(t, carry):
-                attend(t, yy, yy + 1)
-                return carry
-
-            lax.fori_loop(1, 9, one, 0)
-            give(yy)
-
+
+    @pl.when(y == 0)
+    def _():
+        later_pass(1, 2)
+
+    give(1)
+    give(0)
     for d in range(1, 4):
 
         @pl.when(y + d <= 3)
@@ -633,10 +642,10 @@
             pltpu.VMEM((NQ, 128), BF16),
             pltpu.VMEM((2, NQ, 128), BF16),
             pltpu.VMEM((2, NZ, HALF, 128), BF16),
-            pltpu.VMEM((8, HS, 2 * HALF), BF16),
+            pltpu.VMEM((8, VT, 2 * HALF), BF16),
             pltpu.VMEM((4, NQ, 128), BF16),
             pltpu.VMEM((4, HS, NQ), BF16),
-            pltpu.VMEM((4, HS, NQ), F32),
+            pltpu.VMEM((4, ACC, NQ), F32),
             pltpu.VMEM((4, 8, NQ), F32),
             pltpu.VMEM((HALF, 128), jnp.int32),
             pltpu.VMEM((5, 8, NQ), jnp.int32),

time: 153 us -> 145 us (0.948)
  the two profiles are of different devices: /device:TPU:1 before, /device:TPU:9 now
where the time goes in v3:
time: 145 us
  Pallas kernels  139 us (96%)
  local copies, waits for them, and re-layouts  5.83 us (4%)
    pallas_call x1, Pallas kernels, body(): pl.pallas_call(main_kernel, out_shape=jax.ShapeDtypeStruct((ROWS, D), F32...  137 us
    unnamed x18, local copies, waits for them, and re-layouts  5.83 us

profile of v3, /device:TPU:9, one launch (start us, length us, event | category | flops | bytes accessed | tf_op | source)
XLA Modules:
  0.0 145.1 jit_solution(5252465827308861811)
XLA Ops:
  0.6 0.0 copy-start
  0.6 1.7 %copy-done = bf16[256,5120]{1,0:T(8,128)(2,1)S(1)} copy-done((bf16[256,5120]{1,0:T(8,128)(2,1)S(1)}, bf16[256,5120]{1,0:T(8,128)(2,1)}, u32[]{:S(2)}) %copy-start) | copy-done | bytes 2621464
  2.4 0.0 copy-start.3
  2.4 0.9 copy-done.3
  3.3 0.0 copy-start.4
  3.3 0.9 copy-done.4
  4.2 0.0 copy-start.5
  4.2 0.9 copy-done.5
  5.2 0.0 copy-start.6
  5.2 0.7 copy-done.6
  5.8 0.0 copy-start.7
  5.8 0.7 copy-done.7
  6.5 0.0 copy-start.1
  6.5 0.0 copy-start.2
  6.5 0.0 copy-start.8
  6.5 137.1 %attention_tick.1.proj_ref = f32[24,5120]{1,0:T(8,128)S(1)} custom-call(bf16[24,4096]{1,0:T(8,128)(2,1)S(1)} %copy-done.3, bf16[24,4096]{1,0:T(8,128)(2,1)S(1)} %copy-done.4, bf16[24,4096]{1,0:T(8,128)(2,1)S(1)} %copy-done.5, bf16[256,5120]{1,0:T(8,128)(2,1)S(1)} %copy-done, s32[32]{0:T(128)S(1)} %copy-done.6, s32[32]{0:T(128)S(1)} %copy-done.7), custom_call_target="tpu_custom_call" | custom-call | tf_op jit(solution)/shard_map/attention_tick/pallas_call | solution.py:632
  143.5 0.0 copy-done.1
  143.6 0.0 copy-done.2
  143.6 0.0 copy-done.8
  143.6 1.5 %euler_update.1 = (bf16[24,5120]{1,0:T(8,128)(2,1)}, f32[24,5120]{1,0:T(8,128)}) custom-call(f32[24,5120]{1,0:T(8,128)S(1)} %attention_tick.1.proj_ref, f32[30,5120]{1,0:T(8,128)S(1)} %copy-done.1, f32[24,5120]{1,0:T(8,128)S(1)} %copy-done.2, s32[32]{0:T(128)S(1)} %copy-done.8, s32[32]{0:T(128)S(1)} %copy-done.6), custom_call_target="tpu_custom_call" | custom-call | tf_op jit(solution)/shard_map/euler_update/pallas_call | solution.py:681
Async XLA Ops:
  0.6 1.7 %copy-start = (bf16[256,5120]{1,0:T(8,128)(2,1)S(1)}, bf16[256,5120]{1,0:T(8,128)(2,1)}, u32[]{:S(2)}) copy-start(bf16[256,5120]{1,0:T(8,128)(2,1)} %w_ref.1) | copy-start | bytes 7864324
  2.4 0.9 copy-start.3
  3.3 0.9 copy-start.4
  4.2 0.9 copy-start.5
  5.2 0.7 copy-start.6
  5.8 0.7 copy-start.7
  6.5 137.1 %copy-start.1 = (f32[30,5120]{1,0:T(8,128)S(1)}, f32[30,5120]{1,0:T(8,128)}, u32[]{:S(2)}) copy-start(f32[30,5120]{1,0:T(8,128)} %gate_ref.1) | copy-start | bytes 1843204
  6.5 137.1 %copy-start.2 = (f32[24,5120]{1,0:T(8,128)S(1)}, f32[24,5120]{1,0:T(8,128)}, u32[]{:S(2)}) copy-start(f32[24,5120]{1,0:T(8,128)} %lat_ref.1) | copy-start | bytes 1474564
  6.5 137.1 %copy-start.8 = (s32[32]{0:T(128)S(1)}, s32[32]{0:T(128)}, u32[]{:S(2)}) copy-start(s32[32]{0:T(128)} %step_ref.1) | copy-start | bytes 388

commit v4 on v3

--- a/solution.py
+++ b/solution.py
@@ -35,8 +35,8 @@
 
 
 def main_kernel(
-    q_ref, k_ref, v_ref, w_ref, slen_ref, wstart_ref, out_ref,
-    pack, ex_s, ex_r, stage, send_q, send_kv, kv, vt, qbuf, qt, acc, stat, pos_ref, row_ref, wf,
+    q_ref, k_ref, v_ref, w_hbm, slen_ref, wstart_ref, out_ref,
+    w_ref, w_sem, pack, ex_s, ex_r, stage, send_q, send_kv, kv, vt, qbuf, qt, acc, stat, pos_ref, row_ref, wf,
     robuf, rstat, obuf, send_o, att, fs, send_c, recv_c, send_x, recv_x,
     ex_ss, ex_rs, zq_s, zq_r, zk_s, zk_r, xk_s, xk_r, q_s, q_r, wz_s, wz_r, wy_s, wy_r,
     o_s, o_r, st_s, st_r, a_s, a_r, c_s, c_r, x_s, x_r,
@@ -120,14 +120,6 @@
         lax.fori_loop(0, NZ, one, 0)
         return stage[slot].astype(BF16)
 
-    pack_tensor(q_ref, 0)
-    pl.semaphore_wait(barrier, 1 + 3 + 3 + 15 + 16 - jnp.where(quad == x, 1, 0))
-    ex_copy(0).start()
-    pack_tensor(k_ref, 1)
-    ex_copy(1).start()
-    pack_tensor(v_ref, 2)
-    ex_copy(2).start()
-
     side = (zdev(1), zdev(NZ - 1))
 
     def wz_forward(direction, i):
@@ -142,7 +134,7 @@
         rows = pl.ds(pl.multiple_of(i * PIECE, PIECE), PIECE)
         cols = pl.ds(pl.multiple_of(c * CHUNK, 128), CHUNK)
         return copy(
-            w_ref.at[rows, cols], wf.at[c, rows], wz_s.at[direction, i], wz_r.at[direction, i], side[direction]
+            w_hbm.at[rows, cols], wf.at[c, rows], wz_s.at[direction, i], wz_r.at[direction, i], side[direction]
         )
 
     def wy_copy(direction, i, d):
@@ -178,6 +170,17 @@
 
                 for d in range(1, 4):
                     wy_copy(direction, i, d).start()
+
+    own_weight = pltpu.make_async_copy(w_hbm, w_ref, w_sem)
+    own_weight.start()
+    pack_tensor(q_ref, 0)
+    pl.semaphore_wait(barrier, 1 + 3 + 3 + 15 + 16 - jnp.where(quad == x, 1, 0))
+    ex_copy(0).start()
+    weight_start()
+    pack_tensor(k_ref, 1)
+    ex_copy(1).start()
+    pack_tensor(v_ref, 2)
+    ex_copy(2).start()
 
     def zrows(n):
         return pl.ds(pl.multiple_of(n * 48, 16), 48)
@@ -217,9 +220,9 @@
     send_kv[0] = unpack_tensor(1)
     send_kv[1] = unpack_tensor(2)
     start_both_ways(zk_copy)
+    weight_point(0)
     for tensor in range(2):
         kv[tensor, z, zrows(x), :] = send_kv[tensor, zrows(z), :]
-    weight_start()
 
     def xk_copy(n, d):
         part = kv.at[:, n, zrows(x)]
@@ -288,9 +291,8 @@
         def _(d=d):
             q_copy(d).start()
 
-    weight_point(0)
+    weight_point(1)
     spread_pair(1)
-    weight_point(1)
     spread_pair(2)
     weight_point(2)
     spread_pair(3)
@@ -377,14 +379,13 @@
         def _():
             spread_pair(t + 3)
 
-        weight_point(2 * t + 1)
         for n in blocks(t):
             gathered(n)
         za, zb = blocks(t)
         vt[t - 1, pl.ds(0, HS), :] = jnp.concatenate([kv[1, za], kv[1, zb]], axis=0).T
         vt[t - 1, pl.ds(HS, VT - HS), :] = jnp.ones((VT - HS, 2 * HALF), BF16)
         attend(t, y, y + 1)
-        weight_point(2 * t + 2)
+        weight_point(t + 2)
         return carry
 
     lax.fori_loop(1, 9, first_pass, 0)
@@ -458,6 +459,45 @@
     @pl.when(quad == x)
     def _():
         att[z % 4, zrows(x), :] = send_o[zrows(z), :]
+
+    for slot in range(3):
+        ex_copy(slot).wait_send()
+
+    def z_end(d, carry):
+        zq_copy(d).wait_send()
+        zk_copy(d).wait_send()
+        return carry
+
+    lax.fori_loop(1, NZ, z_end, 0)
+
+    def n_end(n, carry):
+        for d in range(1, 4):
+            xk_copy(n, d).wait_send()
+
+        return carry
+
+    lax.fori_loop(0, NZ, n_end, 0)
+
+    def w_end(i, carry):
+        for direction in range(2):
+            wz_forward(direction, i).wait_send()
+            for d in range(1, 4):
+                wy_copy(direction, i, d).wait_send()
+        return carry
+
+    lax.fori_loop(0, NP, w_end, 0)
+    for d in range(1, 4):
+
+        @pl.when(y - d >= 0)
+        def _(d=d):
+            q_copy(d).wait_send()
+
+        @pl.when(y + d <= 3)
+        def _(d=d):
+            for one in o_copy(y + d, d):
+                one.wait_send()
+
+    own_weight.wait()
 
     def wy_wait(n, carry):
         direction, i = n // NP, n % NP
@@ -545,52 +585,20 @@
 
     lax.fori_loop(0, 4, collect, 0)
 
-    for slot in range(3):
-        ex_copy(slot).wait_send()
-
-    def z_end(d, carry):
-        zq_copy(d).wait_send()
-        zk_copy(d).wait_send()
-        return carry
-
-    lax.fori_loop(1, NZ, z_end, 0)
-
-    def n_end(n, carry):
-        for d in range(1, 4):
-            xk_copy(n, d).wait_send()
-
-        @pl.when((n != z) | (quad != x))
-        def _():
-            a_copy(n).wait_send()
-
-        return carry
-
-    lax.fori_loop(0, NZ, n_end, 0)
-
-    def w_end(i, carry):
-        for direction in range(2):
-            wz_forward(direction, i).wait_send()
-            for d in range(1, 4):
-                wy_copy(direction, i, d).wait_send()
-        return carry
-
-    lax.fori_loop(0, NP, w_end, 0)
-    for d in range(1, 4):
-
-        @pl.when(y - d >= 0)
-        def _(d=d):
-            q_copy(d).wait_send()
-
-        @pl.when(y + d <= 3)
-        def _(d=d):
-            for one in o_copy(y + d, d):
-                one.wait_send()
-
     def c_end(n, carry):
         c_copy(n).wait_send()
         return carry
 
     lax.fori_loop(0, 8, c_end, 0)
+
+    def a_end(n, carry):
+        @pl.when((n != z) | (quad != x))
+        def _():
+            a_copy(n).wait_send()
+
+        return carry
+
+    lax.fori_loop(0, NZ, a_end, 0)
 
     def x_end(g, carry):
         for d in range(1, 4):
@@ -632,9 +640,11 @@
     projected = pl.pallas_call(
         main_kernel,
         out_shape=jax.ShapeDtypeStruct((ROWS, D), F32),
-        in_specs=[vmem, vmem, vmem, vmem, smem, smem],
+        in_specs=[vmem, vmem, vmem, pl.BlockSpec(memory_space=pl.ANY), smem, smem],
         out_specs=vmem,
         scratch_shapes=[
+            pltpu.VMEM((256, D), BF16),
+            dma,
             pltpu.VMEM((NZ * ROWS, 128), F32),
             pltpu.VMEM((3, NZ * ROWS, 128), BF16),
             pltpu.VMEM((3, NZ * ROWS, 128), BF16),

time: 145 us -> 141 us (0.972)
  Pallas kernels: 139 us -> 134 us
    pallas_call x1, Pallas kernels: 137 us -> 133 us  [body(): pl.pallas_call(main_kernel, out_shape=jax.ShapeDtypeStruct((ROWS, D), F32...]
where the time goes in v4:
time: 141 us
  Pallas kernels  134 us (95%)
  local copies, waits for them, and re-layouts  5.83 us (4%)
    pallas_call x1, Pallas kernels, body(): pl.pallas_call(main_kernel, out_shape=jax.ShapeDtypeStruct((ROWS, D), F32...  133 us
    unnamed x18, local copies, waits for them, and re-layouts  5.83 us

profile of v4, /device:TPU:9, one launch (start us, length us, event | category | flops | bytes accessed | tf_op | source)
XLA Modules:
  0.0 140.7 jit_solution(13906521444267980156)
XLA Ops:
  0.6 0.0 copy-start
  0.6 1.7 %copy-done = bf16[256,5120]{1,0:T(8,128)(2,1)S(1)} copy-done((bf16[256,5120]{1,0:T(8,128)(2,1)S(1)}, bf16[256,5120]{1,0:T(8,128)(2,1)}, u32[]{:S(2)}) %copy-start) | copy-done | bytes 2621464
  2.4 0.0 copy-start.3
  2.4 0.9 copy-done.3
  3.3 0.0 copy-start.4
  3.3 0.9 copy-done.4
  4.2 0.0 copy-start.5
  4.2 0.9 copy-done.5
  5.2 0.0 copy-start.6
  5.2 0.7 copy-done.6
  5.8 0.0 copy-start.7
  5.8 0.7 copy-done.7
  6.5 0.0 copy-start.1
  6.5 0.0 copy-start.2
  6.5 0.0 copy-start.8
  6.5 132.6 %attention_tick.1.proj_ref = f32[24,5120]{1,0:T(8,128)S(1)} custom-call(bf16[24,4096]{1,0:T(8,128)(2,1)S(1)} %copy-done.3, bf16[24,4096]{1,0:T(8,128)(2,1)S(1)} %copy-done.4, bf16[24,4096]{1,0:T(8,128)(2,1)S(1)} %copy-done.5, bf16[256,5120]{1,0:T(8,128)(2,1)S(1)} %copy-done, s32[32]{0:T(128)S(1)} %copy-done.6, s32[32]{0:T(128)S(1)} %copy-done.7), custom_call_target="tpu_custom_call" | custom-call | tf_op jit(solution)/shard_map/attention_tick/pallas_call | solution.py:640
  139.1 0.0 copy-done.1
  139.1 0.0 copy-done.2
  139.1 0.0 copy-done.8
  139.1 1.5 %euler_update.1 = (bf16[24,5120]{1,0:T(8,128)(2,1)}, f32[24,5120]{1,0:T(8,128)}) custom-call(f32[24,5120]{1,0:T(8,128)S(1)} %attention_tick.1.proj_ref, f32[30,5120]{1,0:T(8,128)S(1)} %copy-done.1, f32[24,5120]{1,0:T(8,128)S(1)} %copy-done.2, s32[32]{0:T(128)S(1)} %copy-done.8, s32[32]{0:T(128)S(1)} %copy-done.6), custom_call_target="tpu_custom_call" | custom-call | tf_op jit(solution)/shard_map/euler_update/pallas_call | solution.py:691
Async XLA Ops:
  0.6 1.7 %copy-start = (bf16[256,5120]{1,0:T(8,128)(2,1)S(1)}, bf16[256,5120]{1,0:T(8,128)(2,1)}, u32[]{:S(2)}) copy-start(bf16[256,5120]{1,0:T(8,128)(2,1)} %w_hbm.1) | copy-start | bytes 7864324
  2.4 0.9 copy-start.3
  3.3 0.9 copy-start.4
  4.2 0.9 copy-start.5
  5.2 0.7 copy-start.6
  5.8 0.7 copy-start.7
  6.5 132.6 %copy-start.1 = (f32[30,5120]{1,0:T(8,128)S(1)}, f32[30,5120]{1,0:T(8,128)}, u32[]{:S(2)}) copy-start(f32[30,5120]{1,0:T(8,128)} %gate_ref.1) | copy-start | bytes 1843204
  6.5 132.6 %copy-start.2 = (f32[24,5120]{1,0:T(8,128)S(1)}, f32[24,5120]{1,0:T(8,128)}, u32[]{:S(2)}) copy-start(f32[24,5120]{1,0:T(8,128)} %lat_ref.1) | copy-start | bytes 1474564
  6.5 132.7 %copy-start.8 = (s32[32]{0:T(128)S(1)}, s32[32]{0:T(128)}, u32[]{:S(2)}) copy-start(s32[32]{0:T(128)} %step_ref.1) | copy-start | bytes 388

commit v5 on v4

--- a/solution.py
+++ b/solution.py
@@ -22,6 +22,7 @@
 CHUNK = 640
 PIECE = 64
 NP = 4
+EARLY = 3
 TILE = 256
 VT = HS + 16
 ACC = HS + 8
@@ -374,7 +375,7 @@
                 for one in o_copy(yy, d):
                     one.start()
 
-    def first_pass(t, carry):
+    def arrive(t):
         @pl.when(t < 6)
         def _():
             spread_pair(t + 3)
@@ -384,11 +385,20 @@
         za, zb = blocks(t)
         vt[t - 1, pl.ds(0, HS), :] = jnp.concatenate([kv[1, za], kv[1, zb]], axis=0).T
         vt[t - 1, pl.ds(HS, VT - HS), :] = jnp.ones((VT - HS, 2 * HALF), BF16)
+
+    def own_step(t, carry):
+        arrive(t)
         attend(t, y, y + 1)
         weight_point(t + 2)
         return carry
 
-    lax.fori_loop(1, 9, first_pass, 0)
+    def full_step(t, carry):
+        arrive(t)
+        attend(t, y, 4)
+        weight_point(t + 2)
+        return carry
+
+    lax.fori_loop(1, EARLY + 1, own_step, 0)
     for d in range(1, 4):
 
         @pl.when(y + d <= 3)
@@ -396,22 +406,19 @@
             q_in(d).wait_recv()
             turn(y + d)
 
-    def later_pass(low, high):
-        def one(t, carry):
-            attend(t, low, high)
-            return carry
-
-        lax.fori_loop(1, 9, one, 0)
-
-    later_pass(jnp.maximum(y + 1, 2), 4)
-    give(3)
-    give(2)
-
-    @pl.when(y == 0)
-    def _():
-        later_pass(1, 2)
-
-    give(1)
+    lax.fori_loop(EARLY + 1, 9, full_step, 0)
+
+    for yy in (3, 2, 1):
+
+        @pl.when(y < yy)
+        def _(yy=yy):
+            def one(t, carry):
+                attend(t, yy, yy + 1)
+                return carry
+
+            lax.fori_loop(1, EARLY + 1, one, 0)
+
+        give(yy)
     give(0)
     for d in range(1, 4):
 

time: 141 us -> 135 us (0.957)
  Pallas kernels: 134 us -> 129 us
    pallas_call x1, Pallas kernels: 133 us -> 127 us  [body(): pl.pallas_call(main_kernel, out_shape=jax.ShapeDtypeStruct((ROWS, D), F32...]
where the time goes in v5:
time: 135 us
  Pallas kernels  129 us (96%)
  local copies, waits for them, and re-layouts  5.83 us (4%)
    pallas_call x1, Pallas kernels, body(): pl.pallas_call(main_kernel, out_shape=jax.ShapeDtypeStruct((ROWS, D), F32...  127 us
    unnamed x18, local copies, waits for them, and re-layouts  5.83 us

profile of v5, /device:TPU:9, one launch (start us, length us, event | category | flops | bytes accessed | tf_op | source)
XLA Modules:
  0.0 135.2 jit_solution(18241677502176867599)
XLA Ops:
  0.6 0.0 copy-start
  0.6 1.7 %copy-done = bf16[256,5120]{1,0:T(8,128)(2,1)S(1)} copy-done((bf16[256,5120]{1,0:T(8,128)(2,1)S(1)}, bf16[256,5120]{1,0:T(8,128)(2,1)}, u32[]{:S(2)}) %copy-start) | copy-done | bytes 2621464
  2.4 0.0 copy-start.3
  2.4 0.9 copy-done.3
  3.3 0.0 copy-start.4
  3.3 0.9 copy-done.4
  4.2 0.0 copy-start.5
  4.2 0.9 copy-done.5
  5.2 0.0 copy-start.6
  5.2 0.7 copy-done.6
  5.8 0.0 copy-start.7
  5.8 0.7 copy-done.7
  6.5 0.0 copy-start.1
  6.5 0.0 copy-start.2
  6.5 0.0 copy-start.8
  6.5 127.2 %attention_tick.1.proj_ref = f32[24,5120]{1,0:T(8,128)S(1)} custom-call(bf16[24,4096]{1,0:T(8,128)(2,1)S(1)} %copy-done.3, bf16[24,4096]{1,0:T(8,128)(2,1)S(1)} %copy-done.4, bf16[24,4096]{1,0:T(8,128)(2,1)S(1)} %copy-done.5, bf16[256,5120]{1,0:T(8,128)(2,1)S(1)} %copy-done, s32[32]{0:T(128)S(1)} %copy-done.6, s32[32]{0:T(128)S(1)} %copy-done.7), custom_call_target="tpu_custom_call" | custom-call | tf_op jit(solution)/shard_map/attention_tick/pallas_call | solution.py:647
  133.7 0.0 copy-done.1
  133.7 0.0 copy-done.2
  133.7 0.0 copy-done.8
  133.7 1.5 %euler_update.1 = (bf16[24,5120]{1,0:T(8,128)(2,1)}, f32[24,5120]{1,0:T(8,128)}) custom-call(f32[24,5120]{1,0:T(8,128)S(1)} %attention_tick.1.proj_ref, f32[30,5120]{1,0:T(8,128)S(1)} %copy-done.1, f32[24,5120]{1,0:T(8,128)S(1)} %copy-done.2, s32[32]{0:T(128)S(1)} %copy-done.8, s32[32]{0:T(128)S(1)} %copy-done.6), custom_call_target="tpu_custom_call" | custom-call | tf_op jit(solution)/shard_map/euler_update/pallas_call | solution.py:698
Async XLA Ops:
  0.6 1.7 %copy-start = (bf16[256,5120]{1,0:T(8,128)(2,1)S(1)}, bf16[256,5120]{1,0:T(8,128)(2,1)}, u32[]{:S(2)}) copy-start(bf16[256,5120]{1,0:T(8,128)(2,1)} %w_hbm.1) | copy-start | bytes 7864324
  2.4 0.9 copy-start.3
  3.3 0.9 copy-start.4
  4.2 0.9 copy-start.5
  5.2 0.7 copy-start.6
  5.8 0.7 copy-start.7
  6.5 127.2 %copy-start.1 = (f32[30,5120]{1,0:T(8,128)S(1)}, f32[30,5120]{1,0:T(8,128)}, u32[]{:S(2)}) copy-start(f32[30,5120]{1,0:T(8,128)} %gate_ref.1) | copy-start | bytes 1843204
  6.5 127.2 %copy-start.2 = (f32[24,5120]{1,0:T(8,128)S(1)}, f32[24,5120]{1,0:T(8,128)}, u32[]{:S(2)}) copy-start(f32[24,5120]{1,0:T(8,128)} %lat_ref.1) | copy-start | bytes 1474564
  6.5 127.2 %copy-start.8 = (s32[32]{0:T(128)S(1)}, s32[32]{0:T(128)}, u32[]{:S(2)}) copy-start(s32[32]{0:T(128)} %step_ref.1) | copy-start | bytes 388

commit v6 on v5

--- a/solution.py
+++ b/solution.py
@@ -22,7 +22,7 @@
 CHUNK = 640
 PIECE = 64
 NP = 4
-EARLY = 3
+EARLY = 2
 TILE = 256
 VT = HS + 16
 ACC = HS + 8
@@ -47,7 +47,8 @@
     y, zlo = span // 8, span % 8
     x, zhi, core = head // 4, (head // 2) % 2, head % 2
     z = zhi * 8 + zlo
-    quad = z // 4
+    quad = (z // 4 + 2 * core) % 4
+    fours = (x + 2 * core) % 4
 
     def copy(src, dst, ssem, rsem, dev):
         return pltpu.make_async_remote_copy(
@@ -82,7 +83,7 @@
     lax.fori_loop(1, NZ, greet_z, 0)
 
     def greet_o(n, carry):
-        sx, sz = n // 4, 4 * x + n % 4
+        sx, sz = n // 4, 4 * fours + n % 4
 
         @pl.when((sx != x) | (sz != z))
         def _():
@@ -94,11 +95,13 @@
 
     def pack_tensor(ref, slot):
         def one(n, carry):
-            col = 128 * (8 * (n // 4) + 4 * ((n // 2) % 2) + n % 2)
+            low = 128 * (4 * ((n // 2) % 2) + n % 2)
+            col = low + 1024 * ((n // 4 + 2 * core) % 4) + 256 * core
+            other = low + 1024 * ((n // 4 + 2 * (1 - core)) % 4) + 256 * (1 - core)
             row = pl.ds(pl.multiple_of(n * ROWS, 8), ROWS)
-            theirs = ref[:, pl.ds(pl.multiple_of(col + 256 * (1 - core), 128), 128)]
+            theirs = ref[:, pl.ds(pl.multiple_of(other, 128), 128)]
             pack[row, :] = theirs.astype(F32)
-            mine = ref[:, pl.ds(pl.multiple_of(col + 256 * core, 128), 128)]
+            mine = ref[:, pl.ds(pl.multiple_of(col, 128), 128)]
             stage[slot, pl.ds(pl.multiple_of(n * 48 + core * ROWS, 8), ROWS), :] = mine.astype(F32)
             return carry
 
@@ -297,6 +300,7 @@
     spread_pair(2)
     weight_point(2)
     spread_pair(3)
+    spread_pair(4)
 
     def turn(yy):
         qt[yy] = qbuf[yy].astype(F32).T.astype(BF16)
@@ -376,9 +380,9 @@
                     one.start()
 
     def arrive(t):
-        @pl.when(t < 6)
+        @pl.when(t < 5)
         def _():
-            spread_pair(t + 3)
+            spread_pair(t + 4)
 
         for n in blocks(t):
             gathered(n)
@@ -449,19 +453,20 @@
     def a_in(n):
         sx = n // 4
         return copy(
-            send_o.at[zrows(n)], att.at[n % 4, zrows(sx)], a_s.at[n], a_r.at[n], place(sx, y, 4 * x + n % 4, core)
-        )
-
-    def a_send(n, carry):
-        to = (z + n) % NZ
-
-        @pl.when((to != z) | (quad != x))
-        def _():
-            a_copy(to).start()
-
-        return carry
-
-    lax.fori_loop(0, NZ, a_send, 0)
+            send_o.at[zrows(n)], att.at[n % 4, zrows(sx)], a_s.at[n], a_r.at[n], place(sx, y, 4 * fours + n % 4, core)
+        )
+
+    def a_send(t, carry):
+        a_copy((z + t) % NZ).start()
+        a_copy((z + NZ - t) % NZ).start()
+        return carry
+
+    lax.fori_loop(1, 8, a_send, 0)
+    a_copy((z + 8) % NZ).start()
+
+    @pl.when(quad != x)
+    def _():
+        a_copy(z).start()
 
     @pl.when(quad == x)
     def _():
@@ -519,7 +524,7 @@
     lax.fori_loop(0, 2 * NP, wy_wait, 0)
 
     def a_wait(n, carry):
-        @pl.when((n // 4 != x) | (4 * x + n % 4 != z))
+        @pl.when((n // 4 != x) | (4 * fours + n % 4 != z))
         def _():
             a_in(n).wait_recv()
 

time: 135 us -> 138 us (1.022)
  Pallas kernels: 129 us -> 131 us
    pallas_call x1, Pallas kernels: 127 us -> 129 us  [body(): pl.pallas_call(main_kernel, out_shape=jax.ShapeDtypeStruct((ROWS, D), F32...]
where the time goes in v6:
time: 138 us; the launch traced here: 137 us
  Pallas kernels  131 us (95%)
  local copies, waits for them, and re-layouts  5.83 us (4%)
    pallas_call x1, Pallas kernels, body(): pl.pallas_call(main_kernel, out_shape=jax.ShapeDtypeStruct((ROWS, D), F32...  129 us
    unnamed x18, local copies, waits for them, and re-layouts  5.83 us

profile of v6, /device:TPU:9, one launch (start us, length us, event | category | flops | bytes accessed | tf_op | source)
XLA Modules:
  0.0 137.3 jit_solution(15831529042975674820)
XLA Ops:
  0.6 0.0 copy-start
  0.6 1.7 %copy-done = bf16[256,5120]{1,0:T(8,128)(2,1)S(1)} copy-done((bf16[256,5120]{1,0:T(8,128)(2,1)S(1)}, bf16[256,5120]{1,0:T(8,128)(2,1)}, u32[]{:S(2)}) %copy-start) | copy-done | bytes 2621464
  2.4 0.0 copy-start.3
  2.4 0.9 copy-done.3
  3.3 0.0 copy-start.4
  3.3 0.9 copy-done.4
  4.2 0.0 copy-start.5
  4.2 0.9 copy-done.5
  5.2 0.0 copy-start.6
  5.2 0.7 copy-done.6
  5.8 0.0 copy-start.7
  5.8 0.7 copy-done.7
  6.5 0.0 copy-start.1
  6.5 0.0 copy-start.2
  6.5 0.0 copy-start.8
  6.5 129.2 %attention_tick.1.proj_ref = f32[24,5120]{1,0:T(8,128)S(1)} custom-call(bf16[24,4096]{1,0:T(8,128)(2,1)S(1)} %copy-done.3, bf16[24,4096]{1,0:T(8,128)(2,1)S(1)} %copy-done.4, bf16[24,4096]{1,0:T(8,128)(2,1)S(1)} %copy-done.5, bf16[256,5120]{1,0:T(8,128)(2,1)S(1)} %copy-done, s32[32]{0:T(128)S(1)} %copy-done.6, s32[32]{0:T(128)S(1)} %copy-done.7), custom_call_target="tpu_custom_call" | custom-call | tf_op jit(solution)/shard_map/attention_tick/pallas_call | solution.py:652
  135.7 0.0 copy-done.1
  135.7 0.0 copy-done.2
  135.7 0.0 copy-done.8
  135.8 1.5 %euler_update.1 = (bf16[24,5120]{1,0:T(8,128)(2,1)}, f32[24,5120]{1,0:T(8,128)}) custom-call(f32[24,5120]{1,0:T(8,128)S(1)} %attention_tick.1.proj_ref, f32[30,5120]{1,0:T(8,128)S(1)} %copy-done.1, f32[24,5120]{1,0:T(8,128)S(1)} %copy-done.2, s32[32]{0:T(128)S(1)} %copy-done.8, s32[32]{0:T(128)S(1)} %copy-done.6), custom_call_target="tpu_custom_call" | custom-call | tf_op jit(solution)/shard_map/euler_update/pallas_call | solution.py:703
Async XLA Ops:
  0.6 1.7 %copy-start = (bf16[256,5120]{1,0:T(8,128)(2,1)S(1)}, bf16[256,5120]{1,0:T(8,128)(2,1)}, u32[]{:S(2)}) copy-start(bf16[256,5120]{1,0:T(8,128)(2,1)} %w_hbm.1) | copy-start | bytes 7864324
  2.4 0.9 copy-start.3
  3.3 0.9 copy-start.4
  4.2 0.9 copy-start.5
  5.2 0.7 copy-start.6
  5.8 0.7 copy-start.7
  6.5 129.3 %copy-start.1 = (f32[30,5120]{1,0:T(8,128)S(1)}, f32[30,5120]{1,0:T(8,128)}, u32[]{:S(2)}) copy-start(f32[30,5120]{1,0:T(8,128)} %gate_ref.1) | copy-start | bytes 1843204
  6.5 129.3 %copy-start.2 = (f32[24,5120]{1,0:T(8,128)S(1)}, f32[24,5120]{1,0:T(8,128)}, u32[]{:S(2)}) copy-start(f32[24,5120]{1,0:T(8,128)} %lat_ref.1) | copy-start | bytes 1474564
  6.5 129.3 %copy-start.8 = (s32[32]{0:T(128)S(1)}, s32[32]{0:T(128)}, u32[]{:S(2)}) copy-start(s32[32]{0:T(128)} %step_ref.1) | copy-start | bytes 388
